TPU v7x, 32 devices: a whole 2x2x4 slice. The times are simulated.
32 devices in a mesh: wide: 8 (over z, x), narrow: 4 (over y, core).
Axes of the slice: x: 2, y: 2, z: 4, core: 2. Of those that a mesh axis runs over, the one named last changes fastest.
Arguments:
- expression: bfloat16 [32768, 7000], P(('wide', 'narrow')), may hold values from -8 to 8
- epsilon: bfloat16 [32768, 100], P(('wide', 'narrow')), may hold values from -5 to 5
- params: bfloat16 [12734464], P(('wide', 'narrow')), as said below
- panels: int32 [4, 7000], replicated, may hold values 0 or 1
- labels: int32 [32768], P(('wide', 'narrow')), may hold values from 0 to 3, as said below
Outputs:
- rebuilt: bfloat16 [32768, 7000], P(('wide', 'narrow'))
- offset: float32 [4, 100], P(None, 'narrow')
- total_loss: float32 [], replicated
- grad_cells: bfloat16 [32768, 7000], P(('wide', 'narrow'))
- grad_params: float32 [12734464], P(('wide', 'narrow'))
- divergence: float32 [], replicated
Inputs may be any that keep to these rules, and one draw needn't show every extreme that they name: labels of the first 4 cells are 0, 1, ... in order, so every condition has a cell; the others are even over conditions. `params`: packed as described; gains near 1.
All inputs are finite; a program needn't handle non-finite values.
Results may differ from a plain program's by a relative error of at most 0.0065.
Values may be sent and summed in bfloat16 or wider, within the bound.
A program may use at most 384 MiB of HBM per device.

v0:
```python
import math

import jax
import jax.numpy as jnp
from jax import lax
from jax.sharding import PartitionSpec as P

G = 7000
H = 800
L = 100
NC = 4


EPSILON_NORM = 1e-05
KL_WEIGHT = 5e-05


def layer_shapes():
    return [
        (G, H),
        (H,),
        (H,),
        (H, H),
        (H,),
        (H,),
        (H, 2 * L),
        (2 * L,),
        (L, H),
        (H,),
        (H,),
        (H, H),
        (H,),
        (H,),
        (H, G),
        (G,),
    ]


def unpack(packed):
    pieces = []
    cursor = 0
    for layer_shape in layer_shapes():
        length = math.prod(layer_shape)
        pieces.append(packed[cursor : cursor + length].reshape(layer_shape))
        cursor = cursor + length
    return pieces


def transpose_times(left, right):
    return lax.dot_general(
        left, right, (((0,), (0,)), ((), ())), preferred_element_type=jnp.float32
    )


def times_transpose(left, right):
    return lax.dot_general(
        left, right, (((1,), (1,)), ((), ())), preferred_element_type=jnp.float32
    )


def norm_forward(values, gain_vec, shift_vec, cell_total):
    column_sums, squares = lax.psum(
        (jnp.sum(values, axis=0), jnp.sum(values * values, axis=0)), ("wide", "narrow")
    )
    centre = column_sums / cell_total
    spread = squares / cell_total - centre * centre
    inverse = lax.rsqrt(spread + EPSILON_NORM)
    normed = (values - centre) * inverse
    affine = gain_vec.astype(jnp.float32) * normed + shift_vec.astype(jnp.float32)
    active = jax.nn.silu(affine)
    return ((normed, inverse, affine), active.astype(jnp.bfloat16))


def norm_backward(d_active, kept, gain_vec, cell_total):
    normed, inverse, affine = kept
    sigma = jax.nn.sigmoid(affine)
    d_affine = d_active * sigma * (1.0 + affine * (1.0 - sigma))
    shift_part = jnp.sum(d_affine, axis=0)
    gain_part = jnp.sum(d_affine * normed, axis=0)
    shift_all, gain_all = lax.psum((shift_part, gain_part), ("wide", "narrow"))
    d_values = (
        gain_vec.astype(jnp.float32)
        * inverse
        * (d_affine - shift_all / cell_total - normed * gain_all / cell_total)
    )
    return (d_values.astype(jnp.bfloat16), gain_part, shift_part)


def shards(expression, epsilon, params, panels, labels):
    cell_rows = expression.shape[0]
    groups = lax.axis_size("narrow")
    cell_total = cell_rows * lax.axis_size("wide") * groups
    weights = unpack(lax.all_gather(params, ("wide", "narrow"), axis=0, tiled=True))
    onehot_low = (labels[:, None] == jnp.arange(NC, dtype=jnp.int32)[None, :]).astype(jnp.bfloat16)
    gene_mask = jnp.dot(onehot_low, panels.astype(jnp.bfloat16), preferred_element_type=jnp.float32)
    panel_sizes = jnp.sum(panels.astype(jnp.float32), axis=1)
    linear_one = jnp.dot(expression, weights[0], preferred_element_type=jnp.float32)
    kept_one, active_one = norm_forward(linear_one, weights[1], weights[2], cell_total)
    linear_two = jnp.dot(active_one, weights[3], preferred_element_type=jnp.float32)
    kept_two, active_two = norm_forward(linear_two, weights[4], weights[5], cell_total)
    head_out = (
        jnp.dot(active_two, weights[6], preferred_element_type=jnp.float32)
        + weights[7].astype(jnp.float32)
    ).astype(jnp.bfloat16)
    latent_mean = head_out[:, :L]
    logvar = head_out[:, L:]
    hot_tiled = jnp.tile(onehot_low, (1, groups))
    col_mean, col_logvar, col_noise, col_hot = (
        lax.all_to_all(latent_mean, "narrow", split_axis=1, concat_axis=0, tiled=True),
        lax.all_to_all(logvar, "narrow", split_axis=1, concat_axis=0, tiled=True),
        lax.all_to_all(epsilon, "narrow", split_axis=1, concat_axis=0, tiled=True),
        lax.all_to_all(hot_tiled, "narrow", split_axis=1, concat_axis=0, tiled=True),
    )
    cond_sums, cond_counts, mean_sums = lax.psum(
        (
            transpose_times(col_hot, col_mean),
            jnp.sum(col_hot.astype(jnp.float32), axis=0),
            jnp.sum(col_mean.astype(jnp.float32), axis=0),
        ),
        "wide",
    )
    offset = cond_sums / cond_counts[:, None] - mean_sums / cell_total
    mean_used = col_mean.astype(jnp.float32)
    logvar_used = col_logvar.astype(jnp.float32)
    noise_used = col_noise.astype(jnp.float32)
    deviation = jnp.exp(0.5 * logvar_used)
    chosen = jnp.dot(col_hot.astype(jnp.float32), offset, precision=lax.Precision.HIGHEST)
    latent_part = (mean_used + deviation * noise_used - chosen).astype(jnp.bfloat16)
    diverge_local = jnp.sum(1.0 + logvar_used - mean_used * mean_used - jnp.exp(logvar_used))
    latent = lax.all_to_all(latent_part, "narrow", split_axis=0, concat_axis=1, tiled=True)
    linear_three = jnp.dot(latent, weights[8], preferred_element_type=jnp.float32)
    kept_three, active_three = norm_forward(linear_three, weights[9], weights[10], cell_total)
    linear_four = jnp.dot(active_three, weights[11], preferred_element_type=jnp.float32)
    kept_four, active_four = norm_forward(linear_four, weights[12], weights[13], cell_total)
    output = jnp.dot(active_four, weights[14], preferred_element_type=jnp.float32) + weights[
        15
    ].astype(jnp.float32)
    rebuilt = jax.nn.softplus(output)
    residue = rebuilt - expression.astype(jnp.float32)
    mask_total = jnp.sum(cond_counts * panel_sizes)
    squared_sum, diverge_sum = lax.psum(
        (jnp.sum(gene_mask * residue * residue), diverge_local), ("wide", "narrow")
    )
    divergence = -0.5 * diverge_sum / cell_total
    total_loss = squared_sum / mask_total + KL_WEIGHT * divergence
    weights = unpack(lax.all_gather(params, ("wide", "narrow"), axis=0, tiled=True))
    direct_term = 2.0 * gene_mask * residue / mask_total
    d_output = (direct_term * jax.nn.sigmoid(output)).astype(jnp.bfloat16)
    grad_out_bias = jnp.sum(d_output.astype(jnp.float32), axis=0)
    grad_dec_out = transpose_times(active_four, d_output)
    d_linear_four, gain_four, shift_four = norm_backward(
        times_transpose(d_output, weights[14]), kept_four, weights[12], cell_total
    )
    grad_dec_two = transpose_times(active_three, d_linear_four)
    d_linear_three, gain_three, shift_three = norm_backward(
        times_transpose(d_linear_four, weights[11]), kept_three, weights[9], cell_total
    )
    grad_dec_one = transpose_times(latent, d_linear_three)
    d_latent = times_transpose(d_linear_three, weights[8]).astype(jnp.bfloat16)
    d_used = lax.all_to_all(d_latent, "narrow", split_axis=1, concat_axis=0, tiled=True)
    cond_grad, total_grad = lax.psum(
        (transpose_times(col_hot, d_used), jnp.sum(d_used.astype(jnp.float32), axis=0)), "wide"
    )
    d_float = d_used.astype(jnp.float32)
    per_condition = jnp.dot(
        col_hot.astype(jnp.float32),
        cond_grad / cond_counts[:, None],
        precision=lax.Precision.HIGHEST,
    )
    d_mean_part = (
        d_float - per_condition + total_grad / cell_total + KL_WEIGHT * mean_used / cell_total
    ).astype(jnp.bfloat16)
    d_logvar_part = (
        0.5 * d_float * deviation * noise_used
        + KL_WEIGHT * 0.5 * (jnp.exp(logvar_used) - 1.0) / cell_total
    ).astype(jnp.bfloat16)
    d_mean, d_logvar = (
        lax.all_to_all(d_mean_part, "narrow", split_axis=0, concat_axis=1, tiled=True),
        lax.all_to_all(d_logvar_part, "narrow", split_axis=0, concat_axis=1, tiled=True),
    )
    d_heads = jnp.concatenate([d_mean, d_logvar], axis=1)
    grad_head_bias = jnp.sum(d_heads.astype(jnp.float32), axis=0)
    grad_heads = transpose_times(active_two, d_heads)
    d_linear_two, gain_two, shift_two = norm_backward(
        times_transpose(d_heads, weights[6]), kept_two, weights[4], cell_total
    )
    grad_enc_two = transpose_times(active_one, d_linear_two)
    d_linear_one, gain_one, shift_one = norm_backward(
        times_transpose(d_linear_two, weights[3]), kept_one, weights[1], cell_total
    )
    grad_cells = (times_transpose(d_linear_one, weights[0]) - direct_term).astype(jnp.bfloat16)
    other_grads = [
        gain_one,
        shift_one,
        grad_enc_two,
        gain_two,
        shift_two,
        grad_heads,
        grad_head_bias,
        grad_dec_one,
        gain_three,
        shift_three,
        grad_dec_two,
        gain_four,
        shift_four,
        grad_dec_out,
        grad_out_bias,
    ]
    flat_total = params.shape[0] * lax.axis_size("wide") * groups
    grad_enc_one = transpose_times(expression, d_linear_one)
    flat_grad = jnp.concatenate(
        [grad_enc_one.reshape(-1)] + [piece.reshape(-1) for piece in other_grads]
    )
    flat_grad = jnp.pad(flat_grad, (0, flat_total - flat_grad.shape[0]))
    grad_params = lax.psum_scatter(flat_grad, ("wide", "narrow"), scatter_dimension=0, tiled=True)
    return (rebuilt.astype(jnp.bfloat16), offset, total_loss, grad_cells, grad_params, divergence)


def solution(mesh):
    in_specs = (
        P(("wide", "narrow"), None),
        P(("wide", "narrow"), None),
        P(("wide", "narrow")),
        P(),
        P(("wide", "narrow")),
    )
    out_specs = (
        P(("wide", "narrow"), None),
        P(None, "narrow"),
        P(),
        P(("wide", "narrow"), None),
        P(("wide", "narrow")),
        P(),
    )
    return jax.shard_map(shards, mesh=mesh, in_specs=in_specs, out_specs=out_specs, check_vma=False)
```

profile of v0, /device:TPU:17, one launch (start us, length us, event | category | flops | bytes accessed | tf_op | source)
XLA Modules:
  0.0 2472.6 jit_solution(7354777934241143270)
XLA Ops:
  22.0 273.7 %all-gather.3.cloned.1.call-done = bf16[32,1,397952]{2,1,0:T(2,128)(2,1)} async-done(((bf16[1,1,397952]{2,1,0:T(2,128)(2,1)}), bf16[32,1,397952]{2,1,0:T(2,128)(2,1)}) %all-gather.3.cloned.1.call-update) | async-done | bytes 25468944 | tf_op jit(solution)/shard_map/all_gather | solution.py:93
  295.7 138.8 %reduce.4 = bf16[32,397952]{1,0:T(8,128)(2,1)} reduce(bf16[32,1,397952]{2,1,0:T(2,128)(2,1)} %all-gather.3.cloned.1.call-done, bf16[]{:T(256)} %constant.68), dimensions={1}, to_apply=%all-gather.reduce_sub_computation | reduce | bytes 50937856 | tf_op jit(solution)/shard_map/all_gather | solution.py:93
  434.5 59.7 %reshape.162 = bf16[12734464]{0:T(1024)(128)(2,1)} reshape(bf16[32,397952]{1,0:T(8,128)(2,1)} %reduce.4) | data formatting | bytes 50937856
  518.8 25.1 %reshape.144 = bf16[7000,800]{1,0:T(8,128)(2,1)} reshape(bf16[5600000]{0:T(1024)(128)(2,1)} %get-tuple-element.65) | data formatting | bytes 22400000 | tf_op jit(solution)/shard_map/reshape | solution.py:44
  567.0 37.2 %all-reduce.9 = (f32[800]{0:T(1024)S(1)}, f32[800]{0:T(1024)S(1)}) all-reduce(f32[800]{0:T(1024)S(1)} %get-tuple-element.21, f32[800]{0:T(1024)S(1)} %get-tuple-element.20), channel_id=1, replica_groups=mesh['wide'=8,'narrow'=4] {'wide','narrow'}, use_global_device_ids=true, to_apply=%region_3.0 | all-reduce | flops 1600 | bytes 12800 | tf_op jit(solution)/shard_map/psum | solution.py:62
  608.1 41.5 %all-reduce.8 = (f32[800]{0:T(1024)S(1)}, f32[800]{0:T(1024)S(1)}) all-reduce(f32[800]{0:T(1024)S(1)} %get-tuple-element.19, f32[800]{0:T(1024)S(1)} %get-tuple-element.18), channel_id=1, replica_groups=mesh['wide'=8,'narrow'=4] {'wide','narrow'}, use_global_device_ids=true, to_apply=%region_7.8 | all-reduce | flops 1600 | bytes 12800 | tf_op jit(solution)/shard_map/psum | solution.py:62
  715.1 20.3 reshape.149
  743.8 42.0 %all-reduce.7 = (f32[800]{0:T(1024)S(1)}, f32[800]{0:T(1024)}) all-reduce(f32[800]{0:T(1024)} %get-tuple-element.17, f32[800]{0:T(1024)} %get-tuple-element.16), channel_id=1, replica_groups=mesh['wide'=8,'narrow'=4] {'wide','narrow'}, use_global_device_ids=true, to_apply=%region_16.17 | all-reduce | flops 1600 | bytes 12800 | tf_op jit(solution)/shard_map/psum | solution.py:62
  793.1 40.3 %all-reduce.6 = (f32[800]{0:T(1024)S(1)}, f32[800]{0:T(1024)S(1)}) all-reduce(f32[800]{0:T(1024)} %get-tuple-element.15, f32[800]{0:T(1024)} %get-tuple-element.14), channel_id=1, replica_groups=mesh['wide'=8,'narrow'=4] {'wide','narrow'}, use_global_device_ids=true, to_apply=%region_20.21 | all-reduce | flops 1600 | bytes 12800 | tf_op jit(solution)/shard_map/psum | solution.py:62
  839.3 57.9 %convert_reduce_fusion = (f32[7000]{0:T(1024)}, bf16[1024,7000]{0,1:T(8,128)(2,1)}, f32[]{:T(128)}, bf16[1024,7000]{0,1:T(8,128)(2,1)}, f32[1024,7000]{0,1:T(8,128)}) fusion(f32[]{:T(128)} %multiply_reduce_fusion.8, bf16[1024,7000]{0,1:T(8,128)(2,1)} %param.5, f32[7000]{0:T(1024)S(1)} %slice_convert_fusion, f32[1024,7000]{0,1:T(8,128)} %fusion.24, ...), kind=kOutput, calls=%fused_computation.3 | convolution fusion | flops 11633656832 | bytes 113246408 | tf_op jit(solution)/shard_map/dot_general | solution.py:135
  897.2 21.0 fusion.44
  918.2 20.8 fusion.38
  939.1 40.5 %all-reduce.5 = (f32[800]{0:T(1024)S(1)}, f32[800]{0:T(1024)S(1)}) all-reduce(f32[800]{0:T(1024)S(1)} %get-tuple-element.13, f32[800]{0:T(1024)S(1)} %get-tuple-element.12), channel_id=1, replica_groups=mesh['wide'=8,'narrow'=4] {'wide','narrow'}, use_global_device_ids=true, to_apply=%region_30.31 | all-reduce | flops 1600 | bytes 12800 | tf_op jit(solution)/shard_map/psum | solution.py:80
  988.5 39.7 %all-reduce.4 = (f32[800]{0:T(1024)S(1)}, f32[800]{0:T(1024)S(1)}) all-reduce(f32[800]{0:T(1024)S(1)} %get-tuple-element.11, f32[800]{0:T(1024)S(1)} %get-tuple-element.10), channel_id=1, replica_groups=mesh['wide'=8,'narrow'=4] {'wide','narrow'}, use_global_device_ids=true, to_apply=%region_34.35 | all-reduce | flops 1600 | bytes 12800 | tf_op jit(solution)/shard_map/psum | solution.py:80
  1079.1 21.8 reshape.155
  1107.3 41.6 %all-reduce.3 = (f32[800]{0:T(1024)S(1)}, f32[800]{0:T(1024)S(1)}) all-reduce(f32[800]{0:T(1024)S(1)} %get-tuple-element.9, f32[800]{0:T(1024)S(1)} %get-tuple-element.8), channel_id=1, replica_groups=mesh['wide'=8,'narrow'=4] {'wide','narrow'}, use_global_device_ids=true, to_apply=%region_41.42 | all-reduce | flops 1600 | bytes 12800 | tf_op jit(solution)/shard_map/psum | solution.py:80
  1162.8 40.7 %all-reduce.2 = (f32[]{:T(128)}, f32[]{:T(128)}, f32[800]{0:T(1024)S(1)}, f32[800]{0:T(1024)S(1)}) all-reduce(f32[]{:T(128)} %get-tuple-element.49, f32[]{:T(128)} %get-tuple-element.22, f32[800]{0:T(1024)S(1)} %get-tuple-element.7, f32[800]{0:T(1024)S(1)} %get-tuple-element.6), channel_id=1, replica_groups=mesh['wide'=8,'narrow'=4] {'wide','narrow'}, use_global_device_ids=true, to_apply=%region_22.23 | all-reduce | flops 1602 | bytes 12816 | tf_op jit(solution)/shard_map/psum | solution.py:141
  1203.5 21.2 convolution_bitcast_fusion
  1224.8 25.5 %copy.24 = f32[7000,800]{1,0:T(8,128)} copy(f32[7000,800]{0,1:T(8,128)} %convolution_bitcast_fusion) | data formatting | bytes 44800000 | tf_op jit(solution)/shard_map/dot_general | solution.py:50
  1250.3 29.4 %reshape.150 = f32[5600000]{0:T(1024)} reshape(f32[7000,800]{1,0:T(8,128)} %copy.24) | data formatting | bytes 44800000 | tf_op jit(solution)/shard_map/reshape | solution.py:212
  1286.8 409.4 %concatenate.7 = f32[12733600]{0:T(1024)} concatenate(f32[5600000]{0:T(1024)} %reshape.150, f32[800]{0:T(1024)} %copy-done.87, f32[800]{0:T(1024)} %copy-done.86, f32[640000]{0:T(1024)} %reshape.151, f32[800]{0:T(1024)} %copy-done.85, f32[800]{0:T(1024)} %copy-done.84, f32[160000]{0:T(1024)S(1)} %reshape.152, f32[200]{0:T(256)} %convert_reduce_fusion.2, f32[80000]{0:T(1024)S(1)} %copy-done.31, ...), dimensions={0} | concatenate | bytes 101868800 | tf_op jit(solution)/shard_map/concatenate | solution.py:211
  1696.2 34.5 %pad.4 = f32[12734464]{0:T(1024)} pad(f32[12733600]{0:T(1024)} %concatenate.7, f32[]{:T(128)} %constant.52.clone.1), padding=0_864 | pad | bytes 101872256 | tf_op jit(solution)/shard_map/jit(_pad)/pad | solution.py:214
  1733.7 48.7 %subtract_convert_fusion = bf16[1024,7000]{0,1:T(8,128)(2,1)} fusion(bf16[7000,800]{1,0:T(8,128)(2,1)} %reshape.144, f32[1024,800]{0,1:T(8,128)} %get-tuple-element.89, f32[1024,800]{0,1:T(8,128)S(1)} %copy-done.12, f32[800]{0:T(1024)S(1)} %copy-done.96, f32[800]{0:T(1024)S(1)} %copy-done.92, f32[800]{0:T(1024)S(1)} %copy-done.90, f32[800]{0:T(1024)S(1)} %copy-done.78, ...), kind=kOutput, calls=%fused_computation.4 | convolution fusion | flops 11575705600 | bytes 103813600 | tf_op jit(solution)/shard_map/dot_general | solution.py:56
  1782.4 677.9 %all-reduce.14.cloned.1.call-done = f32[12734464]{0:T(1024)} async-done(((f32[12734464]{0:T(1024)}), f32[12734464]{0:T(1024)}) %all-reduce.14.cloned.1.call-update) | async-done | bytes 50937872
  (298 shorter events, 242.8 us)
Async XLA Ops:
  7.2 288.5 %all-gather.3.cloned.1.call-start = ((), (), s32[]{:S(2)}) async-start(), calls=%async_computation.8 | async-start | bytes 52529664 | tf_op jit(solution)/shard_map/all_gather | solution.py:93
  17.1 637.3 %all-to-all-start.3 = ((bf16[1024,4,4]{0,2,1:T(4,128)(2,1)}), bf16[1024,4,4]{0,2,1:T(4,128)(2,1)S(1)}, u32[]{:S(2)}, u32[]{:S(2)}) async-start(bf16[1024,4,4]{0,2,1:T(4,128)(2,1)} %tile.2), calls=%async_computation.3 | async-start | bytes 65536 | tf_op jit(solution)/shard_map/all_to_all | solution.py:112
  513.1 91.2 %copy-start.57 = (f32[800]{0:T(1024)}, f32[800]{0:T(1024)S(1)}, u32[]{:S(2)}) copy-start(f32[800]{0:T(1024)S(1)} %get-tuple-element.59) | copy-start | bytes 9604
  513.1 91.2 %copy-start.59 = (f32[800]{0:T(1024)}, f32[800]{0:T(1024)S(1)}, u32[]{:S(2)}) copy-start(f32[800]{0:T(1024)S(1)} %get-tuple-element.60) | copy-start | bytes 9604
  513.1 136.5 %copy-start.61 = (f32[800]{0:T(1024)}, f32[800]{0:T(1024)S(1)}, u32[]{:S(2)}) copy-start(f32[800]{0:T(1024)S(1)} %get-tuple-element.58) | copy-start | bytes 9604
  513.1 136.5 %copy-start.63 = (f32[800]{0:T(1024)}, f32[800]{0:T(1024)S(1)}, u32[]{:S(2)}) copy-start(f32[800]{0:T(1024)S(1)} %get-tuple-element.61) | copy-start | bytes 9604
  513.1 273.6 %copy-start.65 = (f32[800]{0:T(1024)}, f32[800]{0:T(1024)S(1)}, u32[]{:S(2)}) copy-start(f32[800]{0:T(1024)S(1)} %get-tuple-element.57) | copy-start | bytes 9604
  513.1 273.6 %copy-start.67 = (f32[800]{0:T(1024)}, f32[800]{0:T(1024)S(1)}, u32[]{:S(2)}) copy-start(f32[800]{0:T(1024)S(1)} %get-tuple-element.62) | copy-start | bytes 9604
  513.1 321.7 %copy-start.69 = (f32[800]{0:T(1024)}, f32[800]{0:T(1024)S(1)}, u32[]{:S(2)}) copy-start(f32[800]{0:T(1024)S(1)} %get-tuple-element.55) | copy-start | bytes 9604
  513.1 321.7 %copy-start.71 = (f32[800]{0:T(1024)}, f32[800]{0:T(1024)S(1)}, u32[]{:S(2)}) copy-start(f32[800]{0:T(1024)S(1)} %get-tuple-element.56) | copy-start | bytes 9604
  654.4 10.1 all-to-all-start.2
  664.5 16.6 all-to-all-start
  681.1 8.6 all-to-all-start.1
  705.0 36.4 %all-to-all-start.4 = ((bf16[4,1024,25]{1,2,0:T(8,128)(2,1)}), bf16[4,1024,25]{1,2,0:T(8,128)(2,1)S(1)}, u32[]{:S(2)}, u32[]{:S(2)}) async-start(bf16[4,1024,25]{1,2,0:T(8,128)(2,1)} %copy.20), calls=%async_computation.4 | async-start | bytes 524288 | tf_op jit(solution)/shard_map/all_to_all | solution.py:130
  714.0 125.2 %copy-start.52 = (f32[7000]{0:T(1024)}, f32[7000]{0:T(1024)S(1)}, u32[]{:S(2)}) copy-start(f32[7000]{0:T(1024)S(1)} %slice_convert_fusion) | copy-start | bytes 84004
  839.2 58.0 %copy-start.6 = (f32[1024,800]{0,1:T(8,128)S(1)}, f32[1024,800]{0,1:T(8,128)}, u32[]{:S(2)}) copy-start(f32[1024,800]{0,1:T(8,128)} %get-tuple-element.84) | copy-start | bytes 9830404
  839.2 58.0 %copy-start.40 = (f32[800]{0:T(1024)S(1)}, f32[800]{0:T(1024)}, u32[]{:S(2)}) copy-start(f32[800]{0:T(1024)} %copy-done.39) | copy-start | bytes 9604
  839.2 58.0 %copy-start.42 = (f32[800]{0:T(1024)S(1)}, f32[800]{0:T(1024)}, u32[]{:S(2)}) copy-start(f32[800]{0:T(1024)} %copy-done.41) | copy-start | bytes 9604
  839.2 57.9 %copy-start.70 = (f32[800]{0:T(1024)S(1)}, f32[800]{0:T(1024)}, u32[]{:S(2)}) copy-start(f32[800]{0:T(1024)} %copy-done.69) | copy-start | bytes 9604
  918.2 61.4 %copy-start.56 = (f32[800]{0:T(1024)S(1)}, f32[800]{0:T(1024)}, u32[]{:S(2)}) copy-start(f32[800]{0:T(1024)} %get-tuple-element.54) | copy-start | bytes 9604
  1033.3 10.5 all-to-all-start.5
  1044.9 19.9 all-to-all-start.7
  1064.8 36.7 %all-to-all-start.6 = ((bf16[4,1024,25]{1,2,0:T(8,128)(2,1)}), bf16[4,1024,25]{1,2,0:T(8,128)(2,1)}, u32[]{:S(2)}, u32[]{:S(2)}) async-start(bf16[4,1024,25]{1,2,0:T(8,128)(2,1)} %copy.23), calls=%async_computation.6 | async-start | bytes 524288 | tf_op jit(solution)/shard_map/all_to_all | solution.py:178
  1072.4 1387.9 %all-reduce.14.cloned.1.call-start = ((), (), s32[]{:S(2)}) async-start(), calls=%async_computation.9 | async-start | bytes 101875712
  (83 other events, 1294.3 us)
Sparse Core Ops, SparseCore 0:
  16.6 279.0 all-gather.2
  1730.9 729.3 all-reduce.13
where the time goes:
time: 2510 us; the launch traced here: 2470 us
  waiting for transfers between devices  960 us (38%)
  local copies, waits for them, and re-layouts  701 us (28%)
  blocking collectives  349 us (14%)
  matrix products  236 us (9%)
  other arithmetic  164 us (7%)
  starting transfers between devices  41.7 us (2%)
    unnamed x3, waiting for transfers between devices  678 us
    concatenate x1, local copies, waits for them, and re-layouts, shards(): jnp.concatenate([grad_enc_one.reshape(-1)] + [piece.reshape(-1) for piece...  409 us
    all_gather x1, waiting for transfers between devices, shards(): lax.all_gather(params, ('wide', 'narrow'), axis=0, tiled=True)  274 us
    psum x4, blocking collectives, norm_forward(): lax.psum((jnp.sum(values, axis=0), jnp.sum(values * values, axis=0)), ('w...  161 us
    all_gather x1, other arithmetic, shards(): lax.all_gather(params, ('wide', 'narrow'), axis=0, tiled=True)  139 us
    psum x3, blocking collectives, norm_backward(): shift_all, gain_all = lax.psum((shift_part, gain_part), ('wide', 'narrow'))  122 us
    dot_general x6, matrix products, times_transpose(): lax.dot_general(left, right, (((1,), (1,)), ((), ())), preferred_element_...  84.1 us
    unnamed x204, local copies, waits for them, and re-layouts  80 us
  transfers between devices with their start and end apart: 10, of which 4 were waited for; matrix products, arithmetic and copies ran while one was open for 16% of the time, Pallas kernels for 0%

commit v1 on v0

v1 whole, which is shorter than its diff:
```python
import functools

import jax
import jax.numpy as jnp
from jax import lax
from jax.experimental import pallas as pl
from jax.experimental.pallas import tpu as pltpu
from jax.sharding import PartitionSpec as P

G, H, L, NC = 7000, 800, 100, 4
EPSILON_NORM = 1e-05
KL_WEIGHT = 5e-05
F32, BF16 = jnp.float32, jnp.bfloat16
TN = ((0,), (0,))
NN = ((1,), (0,))
NT = ((1,), (1,))
HX = 816


def mm(left, right, dims):
    return lax.dot_general(left, right, (dims, ((), ())), preferred_element_type=F32)


def params_of(limit=56):
    return pltpu.CompilerParams(dimension_semantics=("arbitrary",), vmem_limit_bytes=limit * 2**20)


def output_kernel(part, block, scale, d_ref, a_ref, x_ref, p_ref, h_ref, reb, direct, dg, g_ref, sq, dscr):
    i = pl.program_id(0)
    cells = a_ref.shape[1]

    @pl.when(i == 0)
    def _():
        g_ref[...] = jnp.zeros_like(g_ref)
        sq[...] = jnp.zeros_like(sq)

    lim = G - i * block
    for j in range(block // part):
        r = slice(j * part, (j + 1) * part)
        inside = lax.broadcasted_iota(jnp.int32, (part, 1), 0) + j * part < lim
        w = d_ref[:, r]
        out = mm(w, a_ref[...], TN)
        mask = jnp.where(inside, mm(p_ref[:, r], h_ref[...], TN), 0.0)
        t = jnp.exp(-jnp.abs(out))
        one = 1.0 + t
        soft = jnp.maximum(out, 0.0) + jnp.where(t < 1e-3, t - 0.5 * t * t, jnp.log(one))
        reb[r, :] = soft.astype(BF16)
        res = jnp.where(mask > 0.0, soft - x_ref[r, :].astype(F32), 0.0)
        sq[...] += jnp.sum((res * res).reshape(part // 8, 8, cells), axis=0)
        dr = scale[0] * res
        direct[r, :] = dr.astype(BF16)
        d = (dr * (jnp.where(out >= 0.0, 1.0, t) / one)).astype(BF16)
        lane = lax.broadcasted_iota(jnp.int32, (1, part), 1) + j * part < lim
        dscr[r, :] = d
    lane = lax.broadcasted_iota(jnp.int32, (1, block), 1) < lim
    dg[...] = mm(a_ref[...], dscr[...], NT).astype(BF16)
    g_ref[...] += mm(jnp.where(lane, d_ref[...], jnp.zeros((), BF16)), dscr[...], NN)


def output_layer(D, act, x, panels, hot, scale, block=1024, part=256):
    cells = x.shape[1]
    n = pl.cdiv(G, block)
    rows = lambda: pl.BlockSpec((block, cells), lambda i: (i, 0))
    whole = lambda r, c: pl.BlockSpec((r, c), lambda i: (0, 0))
    return pl.pallas_call(
        functools.partial(output_kernel, part, block),
        grid=(n,),
        out_shape=(jax.ShapeDtypeStruct((G, cells), BF16), jax.ShapeDtypeStruct((G, cells), BF16),
                   jax.ShapeDtypeStruct((HX, G), BF16), jax.ShapeDtypeStruct((HX, cells), F32),
                   jax.ShapeDtypeStruct((8, cells), F32)),
        in_specs=[pl.BlockSpec(memory_space=pltpu.SMEM), pl.BlockSpec((HX, block), lambda i: (0, i)), whole(HX, cells),
                  rows(), pl.BlockSpec((NC, block), lambda i: (0, i)), whole(NC, cells)],
        out_specs=[rows(), rows(), pl.BlockSpec((HX, block), lambda i: (0, i)), whole(HX, cells), whole(8, cells)],
        scratch_shapes=[pltpu.VMEM((block, cells), BF16)],
        compiler_params=params_of(),
        cost_estimate=pl.CostEstimate(flops=6 * G * H * cells, bytes_accessed=70_000_000, transcendentals=3 * G * cells),
        name="output_layer",
    )(scale.reshape(1), D, act, x, panels, hot)


def first_rows_kernel(block, w_ref, x_ref, o_ref):
    i = pl.program_id(0)

    @pl.when(i == 0)
    def _():
        o_ref[...] = jnp.zeros_like(o_ref)

    inside = lax.broadcasted_iota(jnp.int32, (block, 1), 0) < G - i * block
    zero = jnp.zeros((), BF16)

    @pl.when((i + 1) * block <= G)
    def _():
        o_ref[...] += mm(w_ref[...], x_ref[...], TN)

    @pl.when((i + 1) * block > G)
    def _():
        o_ref[...] += mm(jnp.where(inside, w_ref[...], zero), jnp.where(inside, x_ref[...], zero), TN)


def first_linear(F, x, block=1024):
    cells = x.shape[1]
    return pl.pallas_call(
        functools.partial(first_rows_kernel, block),
        grid=(pl.cdiv(G, block),),
        out_shape=jax.ShapeDtypeStruct((H, cells), F32),
        in_specs=[pl.BlockSpec((block, H), lambda i: (i, 0)), pl.BlockSpec((block, cells), lambda i: (i, 0))],
        out_specs=pl.BlockSpec((H, cells), lambda i: (0, 0)),
        compiler_params=params_of(),
        cost_estimate=pl.CostEstimate(flops=2 * G * H * cells, bytes_accessed=30_000_000, transcendentals=0),
        name="first_linear",
    )(F, x)


def last_kernel(x_ref, w_ref, d_ref, t_ref, fg, gc):
    fg[...] = mm(x_ref[...], d_ref[...], NT).astype(BF16)
    gc[...] = (mm(w_ref[...], d_ref[...], NN) - t_ref[...].astype(F32)).astype(BF16)


def last_layer(x, F, d1, direct, frows, block=512):
    cells = x.shape[1]
    rows = lambda c: pl.BlockSpec((block, c), lambda i: (i, 0))
    return pl.pallas_call(
        last_kernel,
        grid=(pl.cdiv(G, block),),
        out_shape=(jax.ShapeDtypeStruct((frows, H), BF16), jax.ShapeDtypeStruct((G, cells), BF16)),
        in_specs=[rows(cells), rows(H), pl.BlockSpec((H, cells), lambda i: (0, 0)), rows(cells)],
        out_specs=[rows(H), rows(cells)],
        compiler_params=params_of(),
        cost_estimate=pl.CostEstimate(flops=4 * G * H * cells, bytes_accessed=70_000_000, transcendentals=0),
        name="last_layer",
    )(x, F, d1, direct)


MESH = pl.DeviceIdType.MESH
FROWS, DROWS = 496, 64
NF = 18
SHARD = 397952
FLATF = 7126600
ALL = (0, 1, 2)


def d_unit(s):
    v = (s * SHARD - FLATF + 111999) // 112000
    return jnp.where(s == NF, 0, jnp.where(s > 31, 51, v))


def place():
    w, n = lax.axis_index("wide"), lax.axis_index("narrow")
    return w // 2, w % 2, n // 2, n % 2


def dev(z, x, y, c):
    return (z * 2 + x, y * 2 + c)


def index(z, x, y, c):
    return (z * 2 + x) * 4 + y * 2 + c


def grd(cond, guard, fn):
    pl.when(cond if guard is None else jnp.logical_and(cond, guard))(fn)


def four(s):
    return jnp.logical_and(s >= NF, (d_unit(s + 1) - d_unit(s)) == 4)


def greet(z, x, y, c, extra=()):
    bar = pltpu.get_barrier_semaphore()
    sig = lambda d: pl.semaphore_signal(bar, inc=1, device_id=d, device_id_type=MESH)
    for d in extra:
        sig(d)
    sig(dev(z, 1 - x, y, c))
    sig(dev(z, x, 1 - y, c))
    sig(dev(z, x, y, 1 - c))

    @pl.when(z > 0)
    def _():
        sig(dev(z - 1, x, y, c))

    @pl.when(z < 3)
    def _():
        sig(dev(z + 1, x, y, c))
    pl.semaphore_wait(bar, len(extra) + 3 + (z > 0).astype(jnp.int32) + (z < 3).astype(jnp.int32))


class Spread:
    def __init__(self, kind, own, buf, send, recv, base=0):
        self.kind, self.own, self.buf, self.send, self.recv = kind, own, buf, send, recv
        self.place = z, x, y, c = place()
        self.sems, self.base, self.started = {}, base, []
        self.XP, self.YP, self.CP = (z, 1 - x, y, c), (z, x, 1 - y, c), (z, x, y, 1 - c)
        self.UP, self.DN = (z + 1, x, y, c), (z - 1, x, y, c)
        self.tags = {0: (0, z, None)}
        for t in (1, 2, 3):
            self.tags[2 * t] = (2 * t, z - t, z >= t)
            self.tags[2 * t + 1] = (2 * t + 1, z + t, z + t <= 3)

    def pieces(self, s, p):
        if self.kind == "F":
            return [] if p == 2 else [(s < NF, FROWS * s, (0, 240)[p], (240, 256)[p])]
        return [(four(s) if p == 2 else s >= NF, 16 * d_unit(s), (0, 32, 48)[p], (32, 16, 16)[p])]

    def rows(self, s, p):
        for cond, base, off, n in self.pieces(s, p):
            yield cond, self.buf.at[pl.ds(pl.multiple_of(base + off, 16), n)], self.own.at[pl.ds(off, n)]

    def copies(self, s, p, key, target, local):
        if not self.pieces(s, p):
            return []
        k = self.base + self.sems.setdefault((key, p), len(self.sems))
        return [(cond, pltpu.make_async_remote_copy(
            src_ref=own if local else dst, dst_ref=dst, send_sem=self.send.at[k], recv_sem=self.recv.at[k],
            device_id=dev(*target), device_id_type=MESH)) for cond, dst, own in self.rows(s, p)]

    def send_to(self, s, parts, key, target, guard=None, local=False):
        for p in parts:
            for cond, cp in self.copies(s, p, key, target, local):
                grd(cond, guard, cp.start)
        self.started.append((s, parts, key, target, guard, local))

    def wait_from(self, s, parts, key, target, guard=None):
        for p in parts:
            for cond, cp in self.copies(s, p, key, target, False):
                grd(cond, guard, cp.wait_recv)

    def begin(self, loc, planes=True, names="ud"):
        z, x, y, c = self.place
        me = index(*self.place)
        self.from_own(names)
        if planes:
            self.spread(0, True)
        self.kept = [(cond, pltpu.make_async_copy(own, dst, loc.at[p])) for p in ALL for cond, dst, own in self.rows(me, p)]
        for cond, cp in self.kept:
            pl.when(cond)(cp.start)

    def from_own(self, names):
        z, x, y, c = self.place
        for p in ALL:
            for name in names:
                to, more = (self.UP, z < 3) if name == "u" else (self.DN, z > 0)
                self.send_to(index(*self.place), (p,), (name, 1), to, more, True)

    def own_in_place(self):
        for cond, cp in self.kept:
            pl.when(cond)(cp.wait)

    def spread(self, tag, local=False):
        _, zz, guard = self.tags[tag]
        z, x, y, c = self.place
        s = index(zz, x, y, c)
        for p in ALL:
            self.send_to(s, (p,), ("x", tag), self.XP, guard, local)
            self.send_to(s, (p,), ("y", tag), self.YP, guard, local)
        self.send_to(s, ALL, ("c0", tag), self.CP, guard, local)

    def along_z(self, t, names="ud", planes=True):
        z, x, y, c = self.place
        for p in ALL:
            for name in names:
                if name == "u":
                    s, ok, frm, to, more = index(z - t, x, y, c), z >= t, self.DN, self.UP, z < 3
                else:
                    s, ok, frm, to, more = index(z + t, x, y, c), z + t <= 3, self.UP, self.DN, z > 0
                self.wait_from(s, (p,), (name, t), frm, ok)
                if t < 3:
                    self.send_to(s, (p,), (name, t + 1), to, jnp.logical_and(ok, more))
        for name in names if planes else "":
            self.spread(2 * t + (name == "d"))

    def flat_parts(self, tag):
        _, zz, guard = self.tags[tag]
        if tag == 0:
            return (guard, guard)
        even = lax.rem(zz + 4, 2) == 0
        return jnp.logical_and(guard, even), jnp.logical_and(guard, jnp.logical_not(even))

    def cross(self, tag):
        _, zz, guard = self.tags[tag]
        z, x, y, c = self.place
        sx, sy = index(zz, 1 - x, y, c), index(zz, x, 1 - y, c)
        second, half = self.flat_parts(tag)
        self.wait_from(sx, ALL, ("x", tag), self.XP, guard)
        self.send_to(sx, (1, 2), ("xy", tag), self.YP, second)
        self.wait_from(sy, ALL, ("y", tag), self.YP, guard)
        self.send_to(sy, (0,), ("yx", tag), self.XP, half)
        self.send_to(sx, ALL, ("c1", tag), self.CP, guard)
        self.send_to(sy, ALL, ("c2", tag), self.CP, guard)

    def diag(self, tag):
        _, zz, guard = self.tags[tag]
        z, x, y, c = self.place
        sd = index(zz, 1 - x, 1 - y, c)
        second, half = self.flat_parts(tag)
        t, name = tag // 2, "ud"[tag % 2]
        both = jnp.logical_and
        if tag:
            frm, to, more = (self.DN, self.UP, z < 3) if name == "u" else (self.UP, self.DN, z > 0)
            self.wait_from(sd, (0,), ("g" + name, t), frm, second)
            self.wait_from(sd, (1, 2), ("g" + name, t), frm, half)
            if t < 3:
                self.send_to(sd, (0,), ("g" + name, t + 1), to, both(second, more))
                self.send_to(sd, (1, 2), ("g" + name, t + 1), to, both(half, more))
        self.wait_from(sd, (1, 2), ("xy", tag), self.YP, second)
        self.wait_from(sd, (0,), ("yx", tag), self.XP, half)
        if tag == 0:
            even = lax.rem(z, 2) == 0
            odd = jnp.logical_not(even)
            for name, to, more in (("u", self.UP, z < 3), ("d", self.DN, z > 0)):
                self.send_to(sd, (0,), ("g" + name, 1), to, both(even, more))
                self.send_to(sd, (1, 2), ("g" + name, 1), to, both(odd, more))
        self.send_to(sd, ALL, ("c3", tag), self.CP, guard)

    def core(self, tag, i):
        _, zz, guard = self.tags[tag]
        z, x, y, c = self.place
        xx, yy = ((x, y), (1 - x, y), (x, 1 - y), (1 - x, 1 - y))[i]
        self.wait_from(index(zz, xx, yy, 1 - c), ALL, ("c%d" % i, tag), self.CP, guard)

    def end(self):
        for s, parts, key, target, guard, local in self.started:
            for p in parts:
                for cond, cp in self.copies(s, p, key, target, local):
                    grd(cond, guard, cp.wait_send)


def first_kernel(fs, x_hbm, ds, F, D, lin, fv, xv, send, recv, loc, fsem, xsem, dsend, drecv, dloc):
    z, x, y, c = place()
    xcopy = pltpu.make_async_copy(x_hbm, xv, xsem)
    xcopy.start()
    net = Spread("F", fs, fv, send, recv)
    late = Spread("D", ds, D, dsend, drecv)
    greet(z, x, y, c)
    net.begin(loc)
    late.begin(dloc)
    lin[...] = jnp.zeros_like(lin)
    out = []

    def store(s, k, guard):
        r = pl.ds(pl.multiple_of(FROWS * s, 16), FROWS)
        cp = pltpu.make_async_copy(fv.at[r], F.at[r], fsem.at[k])
        grd(s < NF, guard, cp.start)
        out.append((s < NF, guard, cp))

    def times(tag, i):
        _, zz, guard = net.tags[tag]
        xx, yy = ((x, y), (1 - x, y), (x, 1 - y), (1 - x, 1 - y))[i]
        m = (zz * 2 + xx) * 2 + yy

        def whole():
            r = pl.ds(pl.multiple_of(2 * FROWS * m, 16), 2 * FROWS)
            lin[...] += mm(fv[r, :], xv[r, :], TN)

        def rest():
            r = pl.ds(14 * FROWS, G - 14 * FROWS)
            lin[...] += mm(fv[r, :], xv[r, :], TN)
        grd(m < 7, guard, whole)
        grd(m == 7, guard, rest)
        k = 8 * tag + 2 * i
        store(2 * m, k, guard)
        store(2 * m + 1, k + 1, guard)

    def finish(tag, cols):
        for i in cols:
            net.core(tag, i)
            times(tag, i)

    def both(name, *tags):
        for n in (net, late):
            for tag in tags:
                getattr(n, name)(tag)

    def settle(tag, cols):
        for i in cols:
            late.core(tag, i)

    both("along_z", 1)
    both("cross", 0)
    both("along_z", 2)
    both("diag", 0)
    both("cross", 2, 3)
    net.own_in_place()
    late.own_in_place()
    xcopy.wait()
    finish(0, (0, 1, 2, 3))
    both("along_z", 3)
    both("diag", 2, 3)
    both("cross", 4, 5)
    finish(2, (0, 1, 2))
    finish(3, (0, 1, 2))
    both("diag", 4, 5)
    both("cross", 6, 7)
    finish(2, (3,))
    finish(3, (3,))
    finish(4, (0, 1, 2))
    finish(5, (0, 1, 2))
    both("diag", 6, 7)
    for tag in (4, 5):
        finish(tag, (3,))
    for tag in (6, 7):
        finish(tag, (0, 1, 2, 3))
    for tag in (0, 2, 3, 4, 5, 6, 7):
        settle(tag, (0, 1, 2, 3))
    net.end()
    late.end()
    for cond, guard, cp in out:
        grd(cond, guard, cp.wait)


def spread_and_first(fslot, dslot, x, cid=1):
    cells = x.shape[1]
    V = pltpu.VMEM
    return pl.pallas_call(
        first_kernel,
        out_shape=(jax.ShapeDtypeStruct((FROWS * NF, H), BF16), jax.ShapeDtypeStruct((HX, G), BF16), jax.ShapeDtypeStruct((H, cells), F32)),
        in_specs=[pl.BlockSpec(memory_space=pl.ANY)] * 3,
        out_specs=[pl.BlockSpec(memory_space=pl.ANY)] * 2 + [pl.BlockSpec(memory_space=V)],
        scratch_shapes=[V((FROWS * NF, H), BF16), V((G, cells), BF16), pltpu.SemaphoreType.DMA((128,)), pltpu.SemaphoreType.DMA((128,)),
                        pltpu.SemaphoreType.DMA((3,)), pltpu.SemaphoreType.DMA((64,)), pltpu.SemaphoreType.DMA,
                        pltpu.SemaphoreType.DMA((192,)), pltpu.SemaphoreType.DMA((192,)), pltpu.SemaphoreType.DMA((3,))],
        compiler_params=pltpu.CompilerParams(collective_id=cid, has_side_effects=True, vmem_limit_bytes=58 * 2**20),
        name="spread_and_first",
    )(fslot, x, dslot)


def slots(p):
    n = 32
    me = lax.axis_index("wide") * 4 + lax.axis_index("narrow")
    ax = ("wide", "narrow")
    head = lax.ppermute(p[-36864:], ax, [(i, i + 1) for i in range(n - 1)])
    tail = lax.ppermute(p[:112000], ax, [(i + 1, i) for i in range(n - 1)])
    ext = jnp.concatenate([head, p, tail, jnp.zeros((112000,), p.dtype)])
    f = lax.dynamic_slice(ext, (jnp.maximum(36864 - 1152 * me, 0),), (FROWS * 800,)).reshape(FROWS, 800)
    off = 36864 + FLATF + 112000 * d_unit(me) - SHARD * me
    d = lax.dynamic_slice(ext, (jnp.clip(off, 0, ext.shape[0] - DROWS * 7000),), (DROWS * 7000,)).reshape(DROWS, 7000)
    return f, d

LP = 128
STEP, UNROLL = 32, 5


def rows_loop(n, fn, step=STEP, unroll=UNROLL):
    def body(i, _):
        for j in range(unroll):
            fn(pl.ds(pl.multiple_of((i * unroll + j) * step, step), step))
        return 0
    lax.fori_loop(0, n // (step * unroll), body, 0)


def silu(u):
    return u * (0.5 + 0.5 * jnp.tanh(0.5 * u))


def by_lanes(v):
    return sum(v[:, 128 * i:128 * i + 128] for i in range(v.shape[1] // 128))


def over_rows(buf):
    return jnp.sum(jnp.transpose(buf), axis=0, keepdims=True)


def along_rows(row):
    return jnp.transpose(jnp.broadcast_to(row, (128, 896)))


def wide(col, cells):
    return jnp.concatenate([col] * (cells // 128), axis=1)


class Sums:
    def __init__(self, bufs, sems):
        self.bufs, self.sems, self.turn = bufs, sems, 0
        self.place = z, x, y, c = place()
        self.spot = x * 4 + y * 2 + c
        self.inside = [(k, lax.bitwise_xor(self.spot, k)) for k in range(1, 8)]
        self.planes = [(k, lax.bitwise_xor(z, k)) for k in range(1, 4)]

    def near_dev(self, q):
        return dev(self.place[0], q // 4, (q // 2) % 2, q % 2)

    def far_dev(self, q):
        return dev(q, *self.place[1:])

    def others(self):
        return [self.near_dev(q) for k, q in self.inside] + [self.far_dev(q) for k, q in self.planes]

    def __call__(self, kind, value, between=None, after=None):
        near, far = self.bufs[kind]
        i, t = self.turn, self.sems
        self.turn += 1
        j = self.count[kind] = self.count.get(kind, -1) + 1 if hasattr(self, "count") else self.first(kind)
        s, f = near.at[j], far.at[j]
        s[self.spot] = value
        cps = [pltpu.make_async_remote_copy(src_ref=s.at[self.spot], dst_ref=s.at[self.spot], send_sem=t[0].at[i, k], recv_sem=t[1].at[i, k],
                                            device_id=self.near_dev(q), device_id_type=MESH) for k, q in self.inside]
        for cp in cps:
            cp.start()
        if between:
            between()
        for cp in cps:
            cp.wait_recv()
        z = self.place[0]
        f[z] = jnp.sum(s[...], axis=0)
        cpz = [pltpu.make_async_remote_copy(src_ref=f.at[z], dst_ref=f.at[z], send_sem=t[2].at[i, k], recv_sem=t[3].at[i, k],
                                            device_id=self.far_dev(q), device_id_type=MESH) for k, q in self.planes]
        for cp in cpz:
            cp.start()
        for cp in cps:
            cp.wait_send()
        if after:
            after()
        for cp in cpz:
            cp.wait()
        return jnp.sum(f[...], axis=0)

    def first(self, kind):
        self.count = {}
        return 0


def sums_scratch(stats, tables):
    V = pltpu.VMEM
    n = stats + tables
    dma = pltpu.SemaphoreType.DMA
    return [V((stats, 8, 2, 896), F32), V((stats, 4, 2, 896), F32), V((max(tables, 1), 8, 8, 128), F32), V((max(tables, 1), 4, 8, 128), F32),
            dma((n, 8)), dma((n, 8)), dma((n, 4)), dma((n, 4))]


def forward_kernel(total, lin1, w2, wh, wd1, wd2, grows, bh, hot, eps,
                   act1o, act2o, act3o, ends, heads, latent, lin2o, lin3o, lin4, stat, table,
                   act1, act2, act3, lin2, lin3, osem, bufs, square, n1, f1, n2, f2, a1, a2, a3, a4):
    z, x, y, c = place()
    sums = Sums({"stat": (n1, f1), "table": (n2, f2)}, (a1, a2, a3, a4))
    cells = lin1.shape[1]
    for i in range(2):
        bufs[i, pl.ds(H, 96), :] = jnp.zeros((96, 128), F32)
    square[...] = jnp.zeros_like(square)
    greet_all(sums.others())

    def stats(lin):
        def one(r):
            v = lin[r, :]
            bufs[0, r, :] = by_lanes(v)
            bufs[1, r, :] = by_lanes(v * v)
        rows_loop(H, one)
        return jnp.concatenate([over_rows(bufs[0]), over_rows(bufs[1])])

    def norm(k, lin, out, between=None, after=None):
        t = sums("stat", stats(lin), between, after)
        centre = t[0:1, :] / total
        inverse = lax.rsqrt(t[1:2, :] / total - centre * centre + EPSILON_NORM)
        stat[pl.ds(2 * k, 1), :] = centre
        stat[pl.ds(2 * k + 1, 1), :] = inverse
        scale = inverse * grows[2 * k:2 * k + 1, :]
        bufs[0] = along_rows(scale)
        bufs[1] = along_rows(grows[2 * k + 1:2 * k + 2, :] - centre * scale)

        def one(r):
            out[r, :] = silu(lin[r, :] * wide(bufs[0, r, :], cells) + wide(bufs[1, r, :], cells)).astype(BF16)
        rows_loop(H, one)

    leaving = []

    def leave(src, dst):
        cp = pltpu.make_async_copy(src, dst, osem.at[len(leaving)])
        cp.start()
        leaving.append(cp)

    norm(0, lin1, act1)
    lin2[...] = mm(w2[...], act1[...], TN)
    leave(act1, act1o)
    leave(lin2, lin2o)
    norm(1, lin2, act2)
    leave(act2, act2o)
    h = (mm(wh[...], act2[...], TN) + bh[...]).astype(BF16)
    heads[...] = h
    mu, lv = h[:LP].astype(F32), h[LP:].astype(F32)
    part = mm(hot[...], h[:LP], NT)
    hf = hot[...].astype(F32)
    lane = lax.broadcasted_iota(jnp.int32, (NC, LP), 1)
    top = jnp.where(lane == LP - 1, jnp.sum(hf, axis=1, keepdims=True), part)
    kl = jnp.sum(jnp.sum(1.0 + lv - mu * mu - jnp.exp(lv), axis=0, keepdims=True), axis=1, keepdims=True)
    low = jnp.where(lax.broadcasted_iota(jnp.int32, (4, LP), 0) == 0, kl, 0.0)

    t = sums("table", jnp.concatenate([top, low]))
    table[...] = t
    cond = t[0:NC, :]
    counts = cond[:, LP - 1:LP]
    cond = jnp.where(lane == LP - 1, 0.0, cond)
    off = cond / counts - jnp.sum(cond, axis=0, keepdims=True) / total
    square[pl.ds(0, NC), :] = off
    offc = jnp.transpose(square[...])
    chosen = sum(offc[:, i:i + 1] * hf[i:i + 1, :] for i in range(NC))
    lat = (mu + jnp.exp(0.5 * lv) * eps[...].astype(F32) - chosen).astype(BF16)
    latent[...] = lat
    lin3[...] = mm(wd1[...], latent[...], TN)
    leave(lin3, lin3o)
    norm(2, lin3, act3)
    leave(act3, act3o)
    lin4[...] = mm(wd2[...], act3[...], TN)

    norm(3, lin4, ends)
    ends[pl.ds(H, 16), :] = jnp.where(lax.broadcasted_iota(jnp.int32, (16, ends.shape[1]), 0) == 0, 1.0, 0.0).astype(BF16)
    for cp in leaving:
        cp.wait()


def greet_all(devices):
    bar = pltpu.get_barrier_semaphore()
    for d in devices:
        pl.semaphore_signal(bar, inc=1, device_id=d, device_id_type=MESH)
    pl.semaphore_wait(bar, len(devices))


def hidden_layers(total, lin1, w2, wh, wd1, wd2, grows, bh, hot, eps, cid=2):
    cells = lin1.shape[1]
    V = pltpu.VMEM
    vm = pl.BlockSpec(memory_space=V)
    hbm = pl.BlockSpec(memory_space=pl.ANY)
    S = jax.ShapeDtypeStruct
    return pl.pallas_call(
        functools.partial(forward_kernel, total),
        out_shape=(S((H, cells), BF16), S((H, cells), BF16), S((H, cells), BF16), S((HX, cells), BF16), S((2 * LP, cells), BF16),
                   S((LP, cells), BF16), S((H, cells), F32), S((H, cells), F32), S((H, cells), F32), S((8, 896), F32),
                   S((8, LP), F32)),
        in_specs=[vm] * 9,
        out_specs=[hbm] * 3 + [vm] * 3 + [hbm] * 2 + [vm] * 3,
        scratch_shapes=[*[V((H, cells), BF16)] * 3, *[V((H, cells), F32)] * 2, pltpu.SemaphoreType.DMA((8,)), V((2, 896, 128), F32), V((LP, LP), F32), *sums_scratch(4, 1)],
        compiler_params=pltpu.CompilerParams(collective_id=cid, has_side_effects=True, vmem_limit_bytes=58 * 2**20),
        name="hidden_layers",
    )(lin1, w2, wh, wd1, wd2, grows, bh, hot, eps)


def backward_kernel(total, g4, lin4, w2, wh, wd1, wd2, grows, stat, latent, heads, hot, eps, table, squares, act1i, act2i, act3i, lin1i, lin2i, lin3i,
                    d1, gw2, gwh, gwd1, gwd2, gbh, gnorm, sums2,
                    act1, act2, act3, lin1, lin2, lin3, isem, pbuf, dbuf, hbuf, bufs, part, square, n1, f1, n2, f2, a1, a2, a3, a4):
    cells = lin4.shape[1]
    sums = Sums({"stat": (n1, f1), "table": (n2, f2)}, (a1, a2, a3, a4))
    comes = {}
    for i, (name, src, dst) in enumerate((("lin3", lin3i, lin3), ("act3", act3i, act3), ("lin2", lin2i, lin2), ("act2", act2i, act2),
                                          ("lin1", lin1i, lin1), ("act1", act1i, act1))):
        comes[name] = pltpu.make_async_copy(src, dst, isem.at[i])
        comes[name].start()
    for i in range(2):
        part[i, pl.ds(H, 96), :] = jnp.zeros((96, 128), F32)
    square[...] = jnp.zeros_like(square)
    greet_all(sums.others())

    def norm(k, g, lin, out, between=None):
        centre, inverse = stat[2 * k:2 * k + 1, :], stat[2 * k + 1:2 * k + 2, :]
        gain, shift = grows[2 * k:2 * k + 1, :], grows[2 * k + 1:2 * k + 2, :]
        bufs[0] = along_rows(inverse)
        bufs[1] = along_rows(-centre * inverse)
        bufs[2] = along_rows(gain)
        bufs[3] = along_rows(shift)

        def one(r):
            n = lin[r, :] * wide(bufs[0, r, :], cells) + wide(bufs[1, r, :], cells)
            u = n * wide(bufs[2, r, :], cells) + wide(bufs[3, r, :], cells)
            s = 0.5 + 0.5 * jnp.tanh(0.5 * u)
            p = g[r, :] * s * (1.0 + u * (1.0 - s))
            pbuf[r, :] = p
            part[0, r, :] = by_lanes(p)
            part[1, r, :] = by_lanes(p * n)
        rows_loop(H, one)
        local = jnp.concatenate([over_rows(part[0]), over_rows(part[1])])
        gnorm[pl.ds(2 * k, 2), :] = local
        t = sums("stat", local, between)
        a = gain * inverse
        b = -a * t[1:2, :] / total
        bufs[0] = along_rows(a)
        bufs[1] = along_rows(b * inverse)
        bufs[2] = along_rows(-b * centre * inverse - a * t[0:1, :] / total)

        def two(r):
            out[r, :] = (pbuf[r, :] * wide(bufs[0, r, :], cells) + lin[r, :] * wide(bufs[1, r, :], cells)
                         + wide(bufs[2, r, :], cells)).astype(BF16)
        rows_loop(H, two)

    norm(3, g4, lin4, dbuf)
    pbuf[...] = mm(wd2[...], dbuf[...], NN)
    comes["lin3"].wait()
    comes["act3"].wait()

    def grads4():
        gwd2[...] = mm(act3[...], dbuf[...], NT).astype(BF16)
    norm(2, pbuf, lin3, hbuf, grads4)
    dl = mm(wd1[...], hbuf[...], NN).astype(BF16)
    cond = mm(hot[...], dl, NT)
    sq = jnp.sum(jnp.sum(squares[...], axis=0, keepdims=True), axis=1, keepdims=True)
    low = jnp.where(lax.broadcasted_iota(jnp.int32, (4, LP), 0) == 0, sq, 0.0)

    def grads3():
        gwd1[...] = mm(latent[...], hbuf[...], NT).astype(BF16)
    t = sums("table", jnp.concatenate([cond, low]), grads3)
    sums2[...] = t
    cond = t[0:NC, :]
    counts = table[0:NC, LP - 1:LP]
    square[pl.ds(0, NC), :] = jnp.sum(cond, axis=0, keepdims=True) / total - cond / counts
    take = jnp.transpose(square[...])
    hf = hot[...].astype(F32)
    change = sum(take[:, i:i + 1] * hf[i:i + 1, :] for i in range(NC))
    mu, lv = heads[pl.ds(0, LP), :].astype(F32), heads[pl.ds(LP, LP), :].astype(F32)
    dl = dl.astype(F32)
    dh = jnp.concatenate([
        dl + change + (KL_WEIGHT / total) * mu,
        0.5 * dl * jnp.exp(0.5 * lv) * eps[...].astype(F32) + (0.5 * KL_WEIGHT / total) * (jnp.exp(lv) - 1.0)]).astype(BF16)
    dbuf[pl.ds(0, 2 * LP), :] = dh
    gbh[...] = mm(jnp.ones((8, cells), BF16), dh, NT)
    pbuf[...] = mm(wh[...], dh, NN)
    comes["lin2"].wait()
    comes["act2"].wait()

    def grads2():
        gwh[...] = mm(act2[...], dbuf[pl.ds(0, 2 * LP), :], NT).astype(BF16)
    norm(1, pbuf, lin2, hbuf, grads2)
    pbuf[...] = mm(w2[...], hbuf[...], NN)
    comes["lin1"].wait()
    comes["act1"].wait()

    def grads1():
        gw2[...] = mm(act1[...], hbuf[...], NT).astype(BF16)
    norm(0, pbuf, lin1, d1, grads1)


def hidden_backward(total, g4, lin4, w2, wh, wd1, wd2, grows, stat, latent, heads, hot, eps, table, squares, acts, lins, cid=3):
    cells = lin4.shape[1]
    V = pltpu.VMEM
    vm = pl.BlockSpec(memory_space=V)
    hbm = pl.BlockSpec(memory_space=pl.ANY)
    S = jax.ShapeDtypeStruct
    return pl.pallas_call(
        functools.partial(backward_kernel, total),
        out_shape=(S((H, cells), BF16), S((H, H), BF16), S((H, 2 * LP), BF16), S((LP, H), BF16), S((H, H), BF16),
                   S((8, 2 * LP), F32), S((8, 896), F32), S((8, LP), F32)),
        in_specs=[vm] * 14 + [hbm] * 6,
        out_specs=[vm] * 8,
        scratch_shapes=[*[V((H, cells), BF16)] * 3, *[V((H, cells), F32)] * 3, pltpu.SemaphoreType.DMA((6,)),
                        V((H, cells), F32), V((H, cells), BF16), V((H, cells), BF16),
                        V((4, 896, 128), F32), V((2, 896, 128), F32), V((LP, LP), F32), *sums_scratch(4, 1)],
        compiler_params=pltpu.CompilerParams(collective_id=cid, has_side_effects=True, vmem_limit_bytes=58 * 2**20),
        name="hidden_backward",
    )(g4, lin4, w2, wh, wd1, wd2, grows, stat, latent, heads, hot, eps, table, squares, *acts, *lins)


ZF, ZD = (0, 1, 2), (2, 3)

def reduce_kernel(FG, DG, fo, do, tF, tD, cF, cD, rF, rD, aF, aD, bF, bD, uF, uD, vF, vD, send, recv, loc):
    z, x, y, c = place()
    bar = pltpu.get_barrier_semaphore()
    sig = lambda d: pl.semaphore_signal(bar, inc=1, device_id=d, device_id_type=MESH)
    XP, YP, CP = (z, 1 - x, y, c), (z, x, 1 - y, c), (z, x, y, 1 - c)
    UP, DN = (z + 1, x, y, c), (z - 1, x, y, c)
    for d in (XP, YP, CP):
        sig(dev(*d))
    @pl.when(z > 0)
    def _(): sig(dev(*DN))
    @pl.when(z < 3)
    def _(): sig(dev(*UP))
    pl.semaphore_wait(bar, 3 + (z > 0).astype(jnp.int32) + (z < 3).astype(jnp.int32))

    sems = {}
    def sem_index(key):
        return sems.setdefault(key, len(sems))
    started = []

    def cases(s, part):
        e = d_unit(s)
        four = jnp.logical_and(s >= NF, (d_unit(s + 1) - e) == 4)
        f, d = s < NF, s >= NF
        if part == "all":
            return [(f, "F", 0, 496, 0), (d, "D", 0, 48, 0), (four, "D", 48, 16, 1)]
        if part == "a":
            return [(f, "F", 0, 240, 0), (d, "D", 0, 32, 0)]
        return [(f, "F", 240, 256, 0), (d, "D", 32, 16, 0), (four, "D", 48, 16, 1)]

    def land(pair, zz, b, col=None):
        buf = pair[0 if b == "F" else 1]
        zi = zz if b == "F" else zz - 2
        return buf.at[zi] if col is None else buf.at[col, zi]

    def grd(cond, guard, fn):
        pl.when(cond if guard is None else jnp.logical_and(cond, guard))(fn)

    def clampz(zz, b):
        return jnp.clip(zz, 0, 2) if b == "F" else jnp.clip(zz, 2, 3)

    def make(s, zz, part, key, target, src_of, dst_of):
        out = []
        for cond, b, off, rows, q in cases(s, part):
            k = sem_index((key, q))
            zc = clampz(zz, b)
            ref, base = src_of(b, zc)
            out.append((cond, pltpu.make_async_remote_copy(
                src_ref=ref.at[pl.ds(off if isinstance(base, int) else pl.multiple_of(base + off, 16), rows)],
                dst_ref=dst_of(b, zc)[0].at[pl.ds(off, rows)],
                send_sem=send.at[k], recv_sem=recv.at[k], device_id=dev(*target), device_id_type=MESH)))
        return out

    def go(guard, *a):
        for cond, cp in make(*a):
            grd(cond, guard, cp.start)
        started.append((guard, a))

    def got(guard, *a):
        for cond, cp in make(*a):
            grd(cond, guard, cp.wait_recv)

    def each(rows, off, fn):
        def body(i, _):
            fn(pl.ds(pl.multiple_of(off + 16 * i, 16), 16))
            return 0
        lax.fori_loop(0, rows // 16, body, 0)

    def total(s, guard, part, zz, dst, terms, out=None):
        for cond, b, off, rows, q in cases(s, part):
            zc = clampz(zz, b)
            def fn(b=b, off=off, rows=rows, zc=zc):
                refs = [t(b, zc)[0] for t in terms]
                def step(r):
                    v = refs[0][r, :].astype(jnp.float32)
                    for ref in refs[1:]:
                        v = v + ref[r, :].astype(jnp.float32)
                    if out is None:
                        dst(b, zc)[0][r, :] = v.astype(jnp.bfloat16)
                    else:
                        out[0 if b == "F" else 1][r, :] = v
                each(rows, off, step)
            grd(cond, guard, fn)

    C, R, A, B, U, V = (cF, cD), (rF, rD), (aF, aD), (bF, bD), (uF, uD), (vF, vD)
    cols = ((x, y), (1 - x, y), (x, 1 - y), (1 - x, 1 - y))
    tags = [(7, z - 3, z >= 3), (6, z + 3, z <= 0), (5, z - 2, z >= 2), (4, z + 2, z <= 1),
            (3, z - 1, z >= 1), (2, z + 1, z <= 2), (0, z, None)]

    def own_rows(s):
        return lambda b, zc: (FG, FROWS * s) if b == "F" else (DG, 16 * d_unit(s))
    on = lambda pair, col=None: (lambda b, zc: (land(pair, zc, b, col), 0))

    for tag, zz, guard in tags:
        for col in (3, 1, 2, 0):
            s = index(zz, *cols[col], 1 - c)
            go(guard, s, zz, "all", ("c", tag, col), CP, own_rows(s), on(C, col))

    order = [(tg, col) for tg in tags for col in (3, 1, 2, 0)]

    def load(k, what):
        (tag, zz, guard), col = order[k]
        s = index(zz, *cols[col], c)
        e = d_unit(s)
        for cond, b, off, rows, q in cases(s, "all"):
            src = FG.at[pl.ds(pl.multiple_of(FROWS * s + off, 16), rows)] if b == "F" else DG.at[pl.ds(pl.multiple_of(16 * e + off, 16), rows)]
            dst = (tF if b == "F" else tD).at[k % 2, pl.ds(off, rows)]
            cp = pltpu.make_async_copy(src, dst, loc.at[k % 2, q])
            grd(cond, guard, cp.start if what == "start" else cp.wait)

    def join(k):
        if k + 1 < len(order):
            load(k + 1, "start")
        load(k, "wait")
        (tag, zz, guard), col = order[k]
        s = index(zz, *cols[col], c)
        got(guard, s, zz, "all", ("c", tag, col), CP, own_rows(s), on(C, col))
        mine = lambda b, zc: ((tF if b == "F" else tD).at[k % 2], 0)
        total(s, guard, "all", zz, on(C, col), [on(C, col), mine])

    def first(i):
        tag, zz, guard = tags[i]
        join(4 * i)
        s = index(zz, *cols[3], c)
        go(guard, s, zz, "a", ("xa", tag), XP, on(C, 3), on(R, 1))
        go(guard, s, zz, "b", ("yb", tag), YP, on(C, 3), on(R, 0))
        for k in (1, 2, 3):
            join(4 * i + k)

    def second(i):
        tag, zz, guard = tags[i]
        sx, sy = index(zz, *cols[1], c), index(zz, *cols[2], c)
        got(guard, sx, zz, "b", ("yb", tag), YP, on(C, 3), on(R, 0))
        total(sx, guard, "b", zz, on(C, 1), [on(C, 1), on(R, 0)])
        go(guard, sx, zz, "all", ("X", tag), XP, on(C, 1), on(A))
        got(guard, sy, zz, "a", ("xa", tag), XP, on(C, 3), on(R, 1))
        total(sy, guard, "a", zz, on(C, 2), [on(C, 2), on(R, 1)])
        go(guard, sy, zz, "all", ("Y", tag), YP, on(C, 2), on(B))

    def third(i):
        tag, zz, guard = tags[i]
        s = index(zz, *cols[0], c)
        got(guard, s, zz, "all", ("X", tag), XP, on(C, 1), on(A))
        got(guard, s, zz, "all", ("Y", tag), YP, on(C, 2), on(B))
        t = {7: 3, 6: 3, 5: 2, 4: 2, 3: 1, 2: 1, 0: 0}[tag]
        base = [on(C, 0), on(A), on(B)]
        if t == 0:
            for cond, frm, pair, key in ((z < 3, UP, U, ("zd", 1)), (z > 0, DN, V, ("zu", 1))):
                got(cond, s, zz, "all", key, frm, on(C, 0), on(pair))
            inner = jnp.logical_and(z > 0, z < 3)
            total(s, inner, "all", zz, None, base + [on(U), on(V)], out=(fo, do))
            total(s, z == 0, "all", zz, None, base + [on(U)], out=(fo, do))
            total(s, z == 3, "all", zz, None, base + [on(V)], out=(fo, do))
            return
        down = tag in (7, 5, 3)
        to, frm, pair, name = (DN, UP, U, "zd") if down else (UP, DN, V, "zu")
        more = (z < 3) if down else (z > 0)
        if t < 3:
            got(jnp.logical_and(guard, more), s, zz, "all", (name, t + 1), frm, on(C, 0), on(pair))
            total(s, jnp.logical_and(guard, more), "all", zz, on(C, 0), base + [on(pair)])
            total(s, jnp.logical_and(guard, jnp.logical_not(more)), "all", zz, on(C, 0), base)
        else:
            total(s, guard, "all", zz, on(C, 0), base)
        go(guard, s, zz, "all", (name, t), to, on(C, 0), on(pair))

    me = index(z, x, y, c)
    @pl.when(me >= NF)
    def _(): fo[...] = jnp.zeros_like(fo)
    do[pl.ds(48, 16), :] = jnp.zeros((16, 7000), jnp.float32)
    @pl.when(me < NF)
    def _(): do[pl.ds(0, 48), :] = jnp.zeros((48, 7000), jnp.float32)
    load(0, "start")
    n = len(tags)
    for i in range(n + 2):
        if i < n:
            first(i)
        if 1 <= i <= n:
            second(i - 1)
        if i >= 2:
            third(i - 2)
    for guard, a in started:
        for cond, cp in make(*a):
            grd(cond, guard, cp.wait_send)

def reduce(FG, DG, cid=2):
    B16 = jnp.bfloat16
    V = pltpu.VMEM
    pair = lambda *lead: [V(lead + (3, FROWS, 800), B16), V(lead + (2, DROWS, 7000), B16)]
    return pl.pallas_call(
        reduce_kernel,
        out_shape=(jax.ShapeDtypeStruct((FROWS, 800), jnp.float32), jax.ShapeDtypeStruct((DROWS, 7000), jnp.float32)),
        in_specs=[pl.BlockSpec(memory_space=pl.ANY)] * 2,
        out_specs=[pl.BlockSpec(memory_space=V)] * 2,
        scratch_shapes=[V((2, FROWS, 800), B16), V((2, DROWS, 7000), B16), *pair(4), *pair(2), *pair(), *pair(), *pair(), *pair(),
                        pltpu.SemaphoreType.DMA((192,)), pltpu.SemaphoreType.DMA((192,)), pltpu.SemaphoreType.DMA((2, 2))],
        compiler_params=pltpu.CompilerParams(collective_id=cid, has_side_effects=True, vmem_limit_bytes=60 * 2**20),
        name="sum_gradients",
    )(FG, DG)

def flatten(fo, do):
    n = 32
    me = lax.axis_index("wide") * 4 + lax.axis_index("narrow")
    ax = ("wide", "narrow")
    nextf = lax.ppermute(fo[:26], ax, [(i + 1, i) for i in range(n - 1)]).reshape(-1)
    nextd = lax.ppermute(do[:6], ax, [(18, 17)]).reshape(-1)
    e = d_unit(me)
    last = 16 * jnp.maximum(d_unit(me + 1) - e - 1, 0)
    prevd = lax.ppermute(lax.dynamic_slice(do, (last, 0), (16, 7000)), ax, [(i, i + 1) for i in range(n - 1)]).reshape(-1)
    ff = fo.reshape(-1)
    a = lax.dynamic_slice(jnp.concatenate([ff, nextf]), (1152 * jnp.minimum(me, 16),), (SHARD,))
    b = jnp.concatenate([ff[19584:381000], nextd[:36536]])
    off = 112000 - (112000 * e + 7126600 - SHARD * me)
    c = lax.dynamic_slice(jnp.concatenate([prevd, do.reshape(-1)]), (jnp.clip(off, 0, 560000 - SHARD),), (SHARD,))
    return jnp.where(me < 17, a, jnp.where(me == 17, b, c))


def allsum(arrays):
    return lax.psum(arrays, ("wide", "narrow"))


def norm_forward(values, gain, shift, total):
    sums, squares = allsum([jnp.sum(values, axis=1), jnp.sum(values * values, axis=1)])
    centre = sums / total
    inverse = lax.rsqrt(squares / total - centre * centre + EPSILON_NORM)
    normed = (values - centre[:, None]) * inverse[:, None]
    affine = gain.astype(F32)[:, None] * normed + shift.astype(F32)[:, None]
    return (normed, inverse, affine), jax.nn.silu(affine).astype(BF16)


def norm_backward(g, kept, gain, total):
    normed, inverse, affine = kept
    sigma = jax.nn.sigmoid(affine)
    p = g * sigma * (1.0 + affine * (1.0 - sigma))
    shift_part = jnp.sum(p, axis=1)
    gain_part = jnp.sum(p * normed, axis=1)
    shift_all, gain_all = allsum([shift_part, gain_part])
    d = (gain.astype(F32) * inverse)[:, None] * (p - (shift_all / total)[:, None] - normed * (gain_all / total)[:, None])
    return d.astype(BF16), gain_part, shift_part


def rows_of(params):
    flat = lax.all_gather(params, ("wide", "narrow"), axis=0, tiled=True)
    F = flat[:FROWS * NF * H].reshape(FROWS * NF, H)
    D = flat[FLATF:]
    D = jnp.pad(D, (0, max(0, HX * G - D.shape[0])))[:HX * G].reshape(HX, G)
    return F, D


def scatter_rows(FG, DG, length):
    flat = jnp.concatenate([FG.astype(F32).reshape(-1)[:FLATF], DG.astype(F32).reshape(-1)])
    flat = jnp.pad(flat, (0, max(0, length - flat.shape[0])))[:length]
    return lax.psum_scatter(flat, ("wide", "narrow"), scatter_dimension=0, tiled=True)


def unpack_rows(F):
    tail = jnp.concatenate([F[8004:8908, 200:], F[8005:8909, :200]], axis=1)
    return [None, F[7000], F[7001], F[7002:7802], F[7802], F[7803], F[7804:8004].reshape(H, 2 * L), F[8004, :200],
            tail[:100], tail[100], tail[101], tail[102:902], tail[902], tail[903]]


def pack_rows(g):
    g = [a.astype(BF16) for a in g]
    row = lambda a: a.reshape(1, -1)
    tail = jnp.concatenate([g[7], row(g[8]), row(g[9]), g[10], row(g[11]), row(g[12])])
    bent = jnp.concatenate([jnp.concatenate([row(g[6]), tail[:, 600:]]), jnp.pad(tail[:, :600], ((0, 1), (0, 0)))], axis=1)
    return jnp.concatenate([row(g[0]), row(g[1]), g[2], row(g[3]), row(g[4]), g[5].reshape(200, 800), bent,
                            jnp.zeros((FROWS * NF - 8909, 800), BF16)])


def by_halves(a, axis):
    wide = [(0, 0)] * a.ndim
    wide[axis] = (0, LP - L)
    return jnp.concatenate([jnp.pad(lax.slice_in_dim(a, i, i + L, axis=axis), wide) for i in (0, L)], axis=axis)


def unhalved(a, axis):
    return jnp.concatenate([lax.slice_in_dim(a, i, i + L, axis=axis) for i in (0, LP)], axis=axis)


def one_hot(labels):
    return (labels[None, :] == jnp.arange(NC, dtype=jnp.int32)[:, None]).astype(BF16)


def fast_step(expression, epsilon, params, panels, labels):
    total = float(expression.shape[0] * 32)
    x = expression.T
    hot = one_hot(labels)
    F, D, lin1 = spread_and_first(*slots(params), x)
    w = unpack_rows(F)
    eps = jnp.pad(epsilon.T, ((0, LP - L), (0, 0)))
    wh = by_halves(w[6], 1)
    bh = by_halves(w[7].astype(F32), 0)[:, None]
    wd1 = jnp.pad(w[8], ((0, LP - L), (0, 0)))
    grows = jnp.pad(jnp.stack([w[i].astype(F32) for i in (1, 2, 4, 5, 9, 10, 12, 13)]), ((0, 0), (0, 896 - H)))
    act1, act2, act3, ends, heads, latent, lin2, lin3, lin4, stat, table = hidden_layers(
        total, lin1, w[3], wh, wd1, w[11], grows, bh, hot, eps)
    counts = table[:NC, LP - 1]
    cond_sums = table[:NC, :L]
    offset = cond_sums / counts[:, None] - jnp.sum(cond_sums, axis=0) / total
    mask_total = jnp.sum(counts * jnp.sum(panels.astype(F32), axis=1))
    rebuilt, direct, DG, g4, squares = output_layer(D, ends, x, panels.astype(BF16), hot, 2.0 / mask_total)
    d1, gw2, gwh, gwd1, gwd2, gbh, gnorm, sums2 = hidden_backward(
        total, g4, lin4, w[3], wh, wd1, w[11], grows, stat, latent, heads, hot, eps, table, squares,
        (act1, act2, act3), (lin1, lin2, lin3))
    FG, grad_cells = last_layer(x, F, d1, direct, FROWS * NF)
    gn = gnorm[:, :H]
    tail = pack_rows([gn[1], gn[0], gw2, gn[3], gn[2], unhalved(gwh, 1), unhalved(gbh[0], 0), gwd1[:L], gn[5], gn[4], gwd2, gn[7], gn[6]])
    FG = lax.dynamic_update_slice(FG, tail, (G, 0))
    grad_params = flatten(*reduce(FG, DG, 4))
    divergence = -0.5 * table[NC, 0] / total
    loss = sums2[NC, 0] / mask_total + KL_WEIGHT * divergence
    columns = L // 4
    mine = lax.dynamic_slice(offset, (0, lax.axis_index("narrow") * columns), (NC, columns))
    return rebuilt.T, mine, loss, grad_cells.T, grad_params, divergence


def general_step(expression, epsilon, params, panels, labels):
    total = expression.shape[0] * lax.axis_size("wide") * lax.axis_size("narrow")
    x = expression.T
    noise = epsilon.T.astype(F32)
    F, D = rows_of(params)
    w = unpack_rows(F)
    hot = one_hot(labels)
    panel_sizes = jnp.sum(panels.astype(F32), axis=1)
    kept1, act1 = norm_forward(first_linear(F, x), w[1], w[2], total)
    kept2, act2 = norm_forward(mm(w[3], act1, TN), w[4], w[5], total)
    heads = (mm(w[6], act2, TN) + w[7].astype(F32)[:, None]).astype(BF16)
    mu, logvar = heads[:L].astype(F32), heads[L:].astype(F32)
    deviation = jnp.exp(0.5 * logvar)
    cond_sums, counts, kl = allsum([
        mm(hot, heads[:L], NT), jnp.sum(hot.astype(F32), axis=1),
        jnp.sum(1.0 + logvar - mu * mu - jnp.exp(logvar)).reshape(1)])
    offset = cond_sums / counts[:, None] - jnp.sum(cond_sums, axis=0) / total
    hotf = hot.astype(F32)
    choose = lambda table: sum(table[i][:, None] * hotf[i][None, :] for i in range(NC))
    latent = (mu + deviation * noise - choose(offset)).astype(BF16)
    kept3, act3 = norm_forward(mm(w[8], latent, TN), w[9], w[10], total)
    kept4, act4 = norm_forward(mm(w[11], act3, TN), w[12], w[13], total)
    mask_total = jnp.sum(counts * panel_sizes)
    ends = jnp.concatenate([act4, jnp.ones((1, act4.shape[1]), BF16), jnp.zeros((HX - H - 1, act4.shape[1]), BF16)])
    rebuilt, direct, DG, g4, squares = output_layer(D, ends, x, panels.astype(BF16), hot, 2.0 / mask_total)
    squared_part = jnp.sum(squares)
    d4, gain4, shift4 = norm_backward(g4[:H], kept4, w[12], total)
    grad_wd2 = mm(act3, d4, NT)
    d3, gain3, shift3 = norm_backward(mm(w[11], d4, NN), kept3, w[9], total)
    grad_wd1 = mm(latent, d3, NT)
    d_latent = mm(w[8], d3, NN).astype(BF16)
    cond_grad, squared = allsum([mm(hot, d_latent, NT), squared_part.reshape(1)])
    dl = d_latent.astype(F32)
    total_grad = jnp.sum(cond_grad, axis=0)
    d_mu = dl - choose(cond_grad / counts[:, None]) + (total_grad / total)[:, None] + KL_WEIGHT * mu / total
    d_logvar = 0.5 * dl * deviation * noise + KL_WEIGHT * 0.5 * (jnp.exp(logvar) - 1.0) / total
    d_heads = jnp.concatenate([d_mu, d_logvar]).astype(BF16)
    grad_bh = jnp.sum(d_heads.astype(F32), axis=1)
    grad_wh = mm(act2, d_heads, NT)
    d2, gain2, shift2 = norm_backward(mm(w[6], d_heads, NN), kept2, w[4], total)
    grad_w2 = mm(act1, d2, NT)
    d1, gain1, shift1 = norm_backward(mm(w[3], d2, NN), kept1, w[1], total)
    FG, grad_cells = last_layer(x, F, d1, direct, FROWS * NF)
    tail = pack_rows([gain1, shift1, grad_w2, gain2, shift2, grad_wh, grad_bh, grad_wd1, gain3, shift3, grad_wd2, gain4, shift4])
    FG = lax.dynamic_update_slice(FG, tail, (G, 0))
    grad_params = scatter_rows(FG, DG, params.shape[0] * lax.axis_size("wide") * lax.axis_size("narrow"))
    divergence = -0.5 * kl[0] / total
    loss = squared[0] / mask_total + KL_WEIGHT * divergence
    columns = L // lax.axis_size("narrow")
    mine = lax.dynamic_slice(offset, (0, lax.axis_index("narrow") * columns), (NC, columns))
    return rebuilt.T, mine, loss, grad_cells.T, grad_params, divergence


def solution(mesh):
    cells = P(("wide", "narrow"), None)
    flat = P(("wide", "narrow"))
    step = fast_step if dict(mesh.shape) == {"wide": 8, "narrow": 4} else general_step
    return jax.shard_map(step, mesh=mesh, in_specs=(cells, cells, flat, P(), flat),
                         out_specs=(cells, P(None, "narrow"), P(), cells, flat, P()), check_vma=False)
```

time: 2510 us -> 638 us (0.25); the launches traced: 2470 us -> 627 us
  waiting for transfers between devices: 960 us -> 5.05 us
  local copies, waits for them, and re-layouts: 701 us -> 67.9 us
  Pallas kernels: 0 us -> 514 us
  blocking collectives: 349 us -> 0 us
  matrix products: 236 us -> 0 us
  other arithmetic: 164 us -> 18 us
  starting transfers between devices: 41.7 us -> 15.5 us
    unnamed x3 -> x0, waiting for transfers between devices: 678 us -> none
    pallas_call x0 -> x6, Pallas kernels: none -> 514 us  [the longest x1 153 us: spread_and_first(): pl.pallas_call(first_kernel, out_shape=(jax.ShapeDtypeStruct((FROWS * NF,...]
    concatenate x1 -> x2, local copies, waits for them, and re-layouts: 409 us -> 24.9 us  [the longest x1 16.4 us: pack_rows(): jnp.concatenate([row(g[0]), row(g[1]), g[2], row(g[3]), row(g[4]), g[5].r...]
    psum x10 -> x0, blocking collectives: 349 us -> none  [the longest x4 161 us: norm_forward(): lax.psum((jnp.sum(values, axis=0), jnp.sum(values * values, axis=0)), ('w...]
    all_gather x1 -> x0, waiting for transfers between devices: 274 us -> none  [shards(): lax.all_gather(params, ('wide', 'narrow'), axis=0, tiled=True)]
    dot_general x23 -> x0, matrix products: 236 us -> none  [the longest x6 84.1 us: times_transpose(): lax.dot_general(left, right, (((1,), (1,)), ((), ())), preferred_element_...]
    all_gather x1 -> x0, other arithmetic: 139 us -> none  [shards(): lax.all_gather(params, ('wide', 'narrow'), axis=0, tiled=True)]
    reshape x12 -> x9, local copies, waits for them, and re-layouts: 119 us -> 16.3 us  [the longest x1 2.69 us: flatten(): do.reshape(-1)]
  transfers between devices with their start and end apart: 10 -> 5, of which waited for: 4 -> 1; matrix products, arithmetic and copies ran while one was open for 16% -> 2% of each run, Pallas kernels for 0% -> 0%
where the time goes in v1:
time: 638 us; the launch traced here: 627 us
  Pallas kernels  514 us (81%)
  local copies, waits for them, and re-layouts  67.9 us (11%)
  other arithmetic  18 us (3%)
  starting transfers between devices  15.5 us (2%)
  between operations  6.92 us (1%)
    pallas_call x1, Pallas kernels, spread_and_first(): pl.pallas_call(first_kernel, out_shape=(jax.ShapeDtypeStruct((FROWS * NF,...  153 us
    pallas_call x1, Pallas kernels, reduce(): pl.pallas_call(reduce_kernel, out_shape=(jax.ShapeDtypeStruct((FROWS, 800...  137 us
    pallas_call x1, Pallas kernels, hidden_backward(): pl.pallas_call(functools.partial(backward_kernel, total), out_shape=(S((H...  65.8 us
    pallas_call x1, Pallas kernels, output_layer(): pl.pallas_call(functools.partial(output_kernel, part, block), grid=(n,),...  65.3 us
    pallas_call x1, Pallas kernels, hidden_layers(): pl.pallas_call(functools.partial(forward_kernel, total), out_shape=(S((H,...  53.9 us
    pallas_call x1, Pallas kernels, last_layer(): pl.pallas_call(last_kernel, grid=(pl.cdiv(G, block),), out_shape=(jax.Sha...  38.1 us
    concatenate x1, local copies, waits for them, and re-layouts, pack_rows(): jnp.concatenate([row(g[0]), row(g[1]), g[2], row(g[3]), row(g[4]), g[5].r...  16.4 us
  transfers between devices with their start and end apart: 5, of which 1 were waited for; matrix products, arithmetic and copies ran while one was open for 2% of the time, Pallas kernels for 0%

profile of v1, /device:TPU:17, one launch (start us, length us, event | category | flops | bytes accessed | tf_op | source)
XLA Modules:
  0.0 627.0 jit_solution(9922175003800701877)
XLA Ops:
  1.7 2.6 collective-permute-start.1
  5.2 3.0 collective-permute-start
  14.5 2.3 reshape.93.ds
  17.3 2.2 reshape.92.fs
  19.5 153.1 %spread_and_first.1 = (bf16[8928,800]{1,0:T(8,128)(2,1)}, bf16[816,7000]{1,0:T(8,128)(2,1)}, f32[800,1024]{1,0:T(8,128)}) custom-call(bf16[496,800]{1,0:T(8,128)(2,1)} %reshape.92.fs, bf16[7000,1024]{1,0:T(8,128)(2,1)} %bitcast.13, bf16[64,7000]{1,0:T(8,128)(2,1)} %reshape.93.ds), custom_call_target="tpu_custom_call" | custom-call | tf_op jit(solution)/shard_map/spread_and_first/pallas_call | solution.py:413
  172.6 2.3 slice.165
  181.7 2.8 slice.161.w2
  186.9 53.9 %hidden_layers.1 = (bf16[800,1024]{1,0:T(8,128)(2,1)}, bf16[800,1024]{1,0:T(8,128)(2,1)}, bf16[800,1024]{1,0:T(8,128)(2,1)}, bf16[816,1024]{1,0:T(8,128)(2,1)}, ...) custom-call(f32[800,1024]{1,0:T(8,128)} %get-tuple-element.37.lin1.l, ...), custom_call_target="tpu_custom_call" | custom-call | tf_op jit(solution)/shard_map/hidden_layers/pallas_call | solution.py:621
  242.9 65.3 %output_layer.1 = (bf16[7000,1024]{1,0:T(8,128)(2,1)}, bf16[7000,1024]{1,0:T(8,128)(2,1)}, bf16[816,7000]{1,0:T(8,128)(2,1)}, f32[816,1024]{1,0:T(8,128)}, f32[8,1024]{1,0:T(8,128)}) custom-call(f32[1]{0:T(128)} %bitcast.5.scale, bf16[816,7000]{1,0:T(8,128)(2,1)} %get-tuple-element.40.d_ref, bf16[816,1024]{1,0:T(8,128)(2,1)} %get-tuple-element.41.a_ref, ...), custom_call_target="tpu_custom_call" | custom-call | flops 34406400000 | bytes 70000000 | tf_op jit(solution)/shard_map/output_layer/pallas_call | solution.py:65
  308.3 65.8 %hidden_backward.1 = (bf16[800,1024]{1,0:T(8,128)(2,1)}, bf16[800,800]{1,0:T(8,128)(2,1)}, bf16[800,256]{1,0:T(8,128)(2,1)}, bf16[128,800]{1,0:T(8,128)(2,1)}, b...) custom-call(f32[816,1024]{1,0:T(8,128)} %get-tuple-element.43.g4, ...), custom_call_target="tpu_custom_call" | custom-call | tf_op jit(solution)/shard_map/hidden_backward/pallas_call | solution.py:732
  375.8 8.4 %concatenate.53 = bf16[904,800]{1,0:T(8,128)(2,1)S(1)} concatenate(bf16[100,800]{1,0:T(8,128)(2,1)S(1)} %slice.189, bf16[1,800]{1,0:T(2,128)(2,1)S(1)} %get-tuple-element.75, bf16[1,800]{1,0:T(2,128)(2,1)S(1)} %get-tuple-element.74, bf16[800,800]{1,0:T(8,128)(2,1)} %get-tuple-element.64, bf16[1,800]{1,0:T(2,128)(2,1)S(1)} %get-tuple-element.73, bf16[1,800]{1,0:T(2,128)(2,1)S(1)} %get-tuple-element.72), dimensions={0} | concatenate | bytes 2892800 | tf_op jit(solution)/shard_map/concatenate | solution.py:1010
  387.1 38.1 %last_layer.1 = (bf16[8928,800]{1,0:T(8,128)(2,1)}, bf16[7000,1024]{1,0:T(8,128)(2,1)}) custom-call(bf16[7000,1024]{1,0:T(8,128)(2,1)} %bitcast.15, bf16[8928,800]{1,0:T(8,128)(2,1)} %get-tuple-element.38.w_ref, bf16[800,1024]{1,0:T(8,128)(2,1)} %get-tuple-element.55.d_ref, bf16[7000,1024]{1,0:T(8,128)(2,1)} %get-tuple-element.56.t_ref), custom_call_target="tpu_custom_call" | custom-call | flops 22937600000 | bytes 70000000 | tf_op jit(solution)/shard_map/last_layer/pallas_call | solution.py:122
  425.3 1.9 fusion.1
  427.2 16.4 %concatenate.56 = bf16[1928,800]{1,0:T(8,128)(2,1)S(1)} concatenate(bf16[1,800]{1,0:T(2,128)(2,1)S(1)} %get-tuple-element.79, bf16[1,800]{1,0:T(2,128)(2,1)S(1)} %get-tuple-element.78, bf16[800,800]{1,0:T(8,128)(2,1)} %get-tuple-element.60, bf16[1,800]{1,0:T(2,128)(2,1)S(1)} %get-tuple-element.77, bf16[1,800]{1,0:T(2,128)(2,1)S(1)} %get-tuple-element.76, ...), dimensions={0} | concatenate | bytes 6169600 | tf_op jit(solution)/shard_map/concatenate | solution.py:1012
  443.6 2.1 constant_dynamic-update-slice_fusion.FG
  445.7 137.4 %sum_gradients.1 = (f32[496,800]{1,0:T(8,128)}, f32[64,7000]{1,0:T(8,128)}) custom-call(bf16[8928,800]{1,0:T(8,128)(2,1)} %constant_dynamic-update-slice_fusion.FG, bf16[816,7000]{1,0:T(8,128)(2,1)} %get-tuple-element.65.DG), custom_call_target="tpu_custom_call" | custom-call | tf_op jit(solution)/shard_map/sum_gradients/pallas_call | solution.py:935
  583.1 2.7 reshape.101
  587.5 2.6 reshape.97
  592.8 1.8 constant_dynamic-slice_fusion
  594.6 6.1 collective-permute-start.4
  602.0 2.5 collective-permute-start.2
  609.1 5.0 collective-permute-done.2
  617.5 2.0 reshape.100
  619.5 4.8 fusion.3
  (71 shorter events, 34.7 us)
Async XLA Ops:
  0.6 13.2 %copy-start.1 = (bf16[397952]{0:T(1024)(128)(2,1)S(1)}, bf16[397952]{0:T(1024)(128)(2,1)}, u32[]{:S(2)}) copy-start(bf16[397952]{0:T(1024)(128)(2,1)} %param.7) | copy-start | bytes 2387716
  1.7 12.1 %collective-permute-start.1 = (bf16[112000]{0:T(1024)(128)(2,1)S(1)}, bf16[112000]{0:T(1024)(128)(2,1)S(1)}, u32[]{:S(2)}, u32[]{:S(2)}) collective-permute-start(bf16[112000]{0:T(1024)(128)(2,1)S(1)} %slice.160), channel_id=1, source_target_pairs={{1,0},{2,1},{3,2},{4,3},{5,4},{6,5},{7,6},{8,7},{9,8},{10,9},{11,1... | collective-permute-start | bytes 672008 | tf_op jit(solution)/shard_map/ppermute | solution.py:431
  5.2 8.6 %collective-permute-start = (bf16[36864]{0:T(1024)(128)(2,1)S(1)}, bf16[36864]{0:T(1024)(128)(2,1)S(1)}, u32[]{:S(2)}, u32[]{:S(2)}) collective-permute-start(bf16[36864]{0:T(1024)(128)(2,1)S(1)} %slice.159), channel_id=1, source_target_pairs={{0,1},{1,2},{2,3},{3,4},{4,5},{5,6},{6,7},{7,8},{8,9},{9,10},{10,1... | collective-permute-start | bytes 221192 | tf_op jit(solution)/shard_map/ppermute | solution.py:430
  176.8 2.8 copy-start.5
  181.7 3.6 copy-start.6
  384.3 1.4 copy-start
  384.3 0.7 copy-start.4
  384.3 1.3 copy-start.2
  387.1 38.1 %slice-start = ((bf16[904,800]{1,0:T(8,128)(2,1)}), bf16[904,600]{1,0:T(8,128)(2,1)S(1)}, s32[]{:S(2)}) async-start(bf16[904,800]{1,0:T(8,128)(2,1)} %copy-done), calls=%async_computation | async-start | bytes 2314240 | tf_op jit(solution)/shard_map/slice | solution.py:1011
  587.5 3.5 copy-start.3
  594.6 22.9 %collective-permute-start.4 = (f32[16,7000]{1,0:T(8,128)}, f32[16,7000]{1,0:T(8,128)}, u32[]{:S(2)}, u32[]{:S(2)}) collective-permute-start(f32[16,7000]{1,0:T(8,128)} %constant_dynamic-slice_fusion), channel_id=1, source_target_pairs={{0,1},{1,2},{2,3},{3,4},{4,5},{5,6},{6,7},{7,8},{8,9},{9,10},{10,1... | collective-permute-start | bytes 1344008 | tf_op jit(solution)/shard_map/ppermute | solution.py:954
  600.7 15.1 %collective-permute-start.3 = (f32[6,7000]{1,0:T(8,128)}, f32[6,7000]{1,0:T(8,128)}, u32[]{:S(2)}, u32[]{:S(2)}) collective-permute-start(f32[6,7000]{1,0:T(8,128)} %slice.198), channel_id=1, source_target_pairs={{18,17}} | collective-permute-start | bytes 504008 | tf_op jit(solution)/shard_map/ppermute | solution.py:951
  602.0 12.1 %collective-permute-start.2 = (f32[26,800]{1,0:T(8,128)S(1)}, f32[26,800]{1,0:T(8,128)}, u32[]{:S(2)}, u32[]{:S(2)}) collective-permute-start(f32[26,800]{1,0:T(8,128)S(1)} %slice.196), channel_id=1, source_target_pairs={{1,0},{2,1},{3,2},{4,3},{5,4},{6,5},{7,6},{8,7},{9,8},{10,9},{11,1... | collective-permute-start | bytes 249608 | tf_op jit(solution)/shard_map/ppermute | solution.py:950

commit v2 on v1

--- a/solution.py
+++ b/solution.py
@@ -140,8 +140,8 @@
 
 
 def d_unit(s):
-    v = (s * SHARD - FLATF + 111999) // 112000
-    return jnp.where(s == NF, 0, jnp.where(s > 31, 51, v))
+    v = lax.shift_right_arithmetic(908 * (s - 19) + 1252, 8)
+    return jnp.where(s <= NF, 0, v)
 
 
 def place():
@@ -162,7 +162,7 @@
 
 
 def four(s):
-    return jnp.logical_and(s >= NF, (d_unit(s + 1) - d_unit(s)) == 4)
+    return lax.bitwise_and(lax.shift_right_arithmetic(0x355b, jnp.clip(s - NF, 0, 13)), 1) == 1
 
 
 def greet(z, x, y, c, extra=()):
@@ -199,74 +199,87 @@
     def pieces(self, s, p):
         if self.kind == "F":
             return [] if p == 2 else [(s < NF, FROWS * s, (0, 240)[p], (240, 256)[p])]
-        return [(four(s) if p == 2 else s >= NF, 16 * d_unit(s), (0, 32, 48)[p], (32, 16, 16)[p])]
+        return [(None, 16 * d_unit(s), (0, 32, 48)[p], (32, 16, 16)[p])]
 
     def rows(self, s, p):
         for cond, base, off, n in self.pieces(s, p):
             yield cond, self.buf.at[pl.ds(pl.multiple_of(base + off, 16), n)], self.own.at[pl.ds(off, n)]
 
-    def copies(self, s, p, key, target, local):
-        if not self.pieces(s, p):
-            return []
+    def copy(self, s, p, key, target, local=False):
         k = self.base + self.sems.setdefault((key, p), len(self.sems))
-        return [(cond, pltpu.make_async_remote_copy(
-            src_ref=own if local else dst, dst_ref=dst, send_sem=self.send.at[k], recv_sem=self.recv.at[k],
-            device_id=dev(*target), device_id_type=MESH)) for cond, dst, own in self.rows(s, p)]
-
-    def send_to(self, s, parts, key, target, guard=None, local=False):
-        for p in parts:
-            for cond, cp in self.copies(s, p, key, target, local):
-                grd(cond, guard, cp.start)
-        self.started.append((s, parts, key, target, guard, local))
-
-    def wait_from(self, s, parts, key, target, guard=None):
-        for p in parts:
-            for cond, cp in self.copies(s, p, key, target, False):
-                grd(cond, guard, cp.wait_recv)
+        (_, dst, own), = self.rows(s, p)
+        return pltpu.make_async_remote_copy(src_ref=own if local else dst, dst_ref=dst, send_sem=self.send.at[k],
+                                            recv_sem=self.recv.at[k], device_id=dev(*target), device_id_type=MESH)
+
+    def where(self, s, guard, fn):
+        def last():
+            fn((2,))
+
+        def both():
+            fn((0, 1))
+            if self.kind == "D":
+                pl.when(four(s))(last)
+        grd(s < NF if self.kind == "F" else s >= NF, guard, both)
+
+    def sends(self, s, guard, legs, local=False):
+        def start(what, ps):
+            for p in ps:
+                for parts, key, target, more in legs:
+                    if p in parts:
+                        fn = getattr(self.copy(s, p, key, target, local), what)
+                        fn() if more is None else pl.when(more)(fn)
+        self.started.append((s, guard, functools.partial(start, "wait_send")))
+        return functools.partial(start, "start")
+
+    def gets(self, s, parts, key, target, more=None):
+        def wait(ps):
+            for p in ps:
+                if p in parts:
+                    fn = self.copy(s, p, key, target).wait_recv
+                    fn() if more is None else pl.when(more)(fn)
+        return wait
 
     def begin(self, loc, planes=True, names="ud"):
         z, x, y, c = self.place
         me = index(*self.place)
-        self.from_own(names)
-        if planes:
-            self.spread(0, True)
-        self.kept = [(cond, pltpu.make_async_copy(own, dst, loc.at[p])) for p in ALL for cond, dst, own in self.rows(me, p)]
-        for cond, cp in self.kept:
-            pl.when(cond)(cp.start)
-
-    def from_own(self, names):
-        z, x, y, c = self.place
-        for p in ALL:
-            for name in names:
-                to, more = (self.UP, z < 3) if name == "u" else (self.DN, z > 0)
-                self.send_to(index(*self.place), (p,), (name, 1), to, more, True)
+        fs = [self.sends(me, None, [(ALL, (name, 1), *((self.UP, z < 3) if name == "u" else (self.DN, z > 0)))], True) for name in names]
+        fs += [self.planes(0, True)] if planes else []
+        self.where(me, None, lambda ps: [f(ps) for f in fs])
+
+        def start(what, ps):
+            for p in ps:
+                (_, dst, own), = self.rows(me, p)
+                getattr(pltpu.make_async_copy(own, dst, loc.at[p]), what)()
+        self.kept = lambda: self.where(me, None, functools.partial(start, "wait"))
+        self.where(me, None, functools.partial(start, "start"))
 
     def own_in_place(self):
-        for cond, cp in self.kept:
-            pl.when(cond)(cp.wait)
-
-    def spread(self, tag, local=False):
+        self.kept()
+
+    def planes(self, tag, local=False):
         _, zz, guard = self.tags[tag]
         z, x, y, c = self.place
         s = index(zz, x, y, c)
-        for p in ALL:
-            self.send_to(s, (p,), ("x", tag), self.XP, guard, local)
-            self.send_to(s, (p,), ("y", tag), self.YP, guard, local)
-        self.send_to(s, ALL, ("c0", tag), self.CP, guard, local)
-
-    def along_z(self, t, names="ud", planes=True):
+        return self.sends(s, guard, [(ALL, ("x", tag), self.XP, None), (ALL, ("y", tag), self.YP, None),
+                                     (ALL, ("c0", tag), self.CP, None)], local)
+
+    def along_z(self, t):
         z, x, y, c = self.place
-        for p in ALL:
-            for name in names:
-                if name == "u":
-                    s, ok, frm, to, more = index(z - t, x, y, c), z >= t, self.DN, self.UP, z < 3
-                else:
-                    s, ok, frm, to, more = index(z + t, x, y, c), z + t <= 3, self.UP, self.DN, z > 0
-                self.wait_from(s, (p,), (name, t), frm, ok)
-                if t < 3:
-                    self.send_to(s, (p,), (name, t + 1), to, jnp.logical_and(ok, more))
-        for name in names if planes else "":
-            self.spread(2 * t + (name == "d"))
+        for name in "ud":
+            tag = 2 * t + (name == "d")
+            _, zz, ok = self.tags[tag]
+            frm, to, more = (self.DN, self.UP, z < 3) if name == "u" else (self.UP, self.DN, z > 0)
+            s = index(zz, x, y, c)
+            fs = [self.sends(s, ok, [(ALL, (name, t + 1), to, more)])] if t < 3 else []
+            fs.append(self.planes(tag))
+            get = self.gets(s, ALL, (name, t), frm)
+
+            def fn(ps):
+                for p in ps:
+                    get((p,))
+                    for f in fs:
+                        f((p,))
+            self.where(s, ok, fn)
 
     def flat_parts(self, tag):
         _, zz, guard = self.tags[tag]
@@ -278,14 +291,17 @@
     def cross(self, tag):
         _, zz, guard = self.tags[tag]
         z, x, y, c = self.place
-        sx, sy = index(zz, 1 - x, y, c), index(zz, x, 1 - y, c)
         second, half = self.flat_parts(tag)
-        self.wait_from(sx, ALL, ("x", tag), self.XP, guard)
-        self.send_to(sx, (1, 2), ("xy", tag), self.YP, second)
-        self.wait_from(sy, ALL, ("y", tag), self.YP, guard)
-        self.send_to(sy, (0,), ("yx", tag), self.XP, half)
-        self.send_to(sx, ALL, ("c1", tag), self.CP, guard)
-        self.send_to(sy, ALL, ("c2", tag), self.CP, guard)
+        for s, name, frm, parts, leg, cond, core in (
+                (index(zz, 1 - x, y, c), "x", self.XP, (1, 2), ("xy", tag, self.YP), second, "c1"),
+                (index(zz, x, 1 - y, c), "y", self.YP, (0,), ("yx", tag, self.XP), half, "c2")):
+            get = self.gets(s, ALL, (name, tag), frm)
+            send = self.sends(s, guard, [(parts, leg[:2], leg[2], cond), (ALL, (core, tag), self.CP, None)])
+
+            def fn(ps):
+                get(ps)
+                send(ps)
+            self.where(s, guard, fn)
 
     def diag(self, tag):
         _, zz, guard = self.tags[tag]
@@ -293,35 +309,37 @@
         sd = index(zz, 1 - x, 1 - y, c)
         second, half = self.flat_parts(tag)
         t, name = tag // 2, "ud"[tag % 2]
-        both = jnp.logical_and
+        both = lambda a, b: b if a is None else jnp.logical_and(a, b)
+        gets, legs = [], []
         if tag:
             frm, to, more = (self.DN, self.UP, z < 3) if name == "u" else (self.UP, self.DN, z > 0)
-            self.wait_from(sd, (0,), ("g" + name, t), frm, second)
-            self.wait_from(sd, (1, 2), ("g" + name, t), frm, half)
+            gets = [self.gets(sd, (0,), ("g" + name, t), frm, second), self.gets(sd, (1, 2), ("g" + name, t), frm, half)]
             if t < 3:
-                self.send_to(sd, (0,), ("g" + name, t + 1), to, both(second, more))
-                self.send_to(sd, (1, 2), ("g" + name, t + 1), to, both(half, more))
-        self.wait_from(sd, (1, 2), ("xy", tag), self.YP, second)
-        self.wait_from(sd, (0,), ("yx", tag), self.XP, half)
-        if tag == 0:
+                legs = [((0,), ("g" + name, t + 1), to, both(second, more)), ((1, 2), ("g" + name, t + 1), to, both(half, more))]
+        else:
             even = lax.rem(z, 2) == 0
             odd = jnp.logical_not(even)
             for name, to, more in (("u", self.UP, z < 3), ("d", self.DN, z > 0)):
-                self.send_to(sd, (0,), ("g" + name, 1), to, both(even, more))
-                self.send_to(sd, (1, 2), ("g" + name, 1), to, both(odd, more))
-        self.send_to(sd, ALL, ("c3", tag), self.CP, guard)
+                legs += [((0,), ("g" + name, 1), to, both(even, more)), ((1, 2), ("g" + name, 1), to, both(odd, more))]
+        gets += [self.gets(sd, (1, 2), ("xy", tag), self.YP, second), self.gets(sd, (0,), ("yx", tag), self.XP, half)]
+        send = self.sends(sd, guard, legs + [(ALL, ("c3", tag), self.CP, None)])
+
+        def fn(ps):
+            for get in gets:
+                get(ps)
+            send(ps)
+        self.where(sd, guard, fn)
 
     def core(self, tag, i):
         _, zz, guard = self.tags[tag]
         z, x, y, c = self.place
         xx, yy = ((x, y), (1 - x, y), (x, 1 - y), (1 - x, 1 - y))[i]
-        self.wait_from(index(zz, xx, yy, 1 - c), ALL, ("c%d" % i, tag), self.CP, guard)
+        s = index(zz, xx, yy, 1 - c)
+        self.where(s, guard, self.gets(s, ALL, ("c%d" % i, tag), self.CP))
 
     def end(self):
-        for s, parts, key, target, guard, local in self.started:
-            for p in parts:
-                for cond, cp in self.copies(s, p, key, target, local):
-                    grd(cond, guard, cp.wait_send)
+        for s, guard, fn in self.started:
+            self.where(s, guard, fn)
 
 
 def first_kernel(fs, x_hbm, ds, F, D, lin, fv, xv, send, recv, loc, fsem, xsem, dsend, drecv, dloc):
@@ -632,8 +650,8 @@
 
 
 def backward_kernel(total, g4, lin4, w2, wh, wd1, wd2, grows, stat, latent, heads, hot, eps, table, squares, act1i, act2i, act3i, lin1i, lin2i, lin3i,
-                    d1, gw2, gwh, gwd1, gwd2, gbh, gnorm, sums2,
-                    act1, act2, act3, lin1, lin2, lin3, isem, pbuf, dbuf, hbuf, bufs, part, square, n1, f1, n2, f2, a1, a2, a3, a4):
+                    d1, tail, sums2,
+                    gnorm, rows, upper, lower, gwh, gwl, act1, act2, act3, lin1, lin2, lin3, isem, pbuf, dbuf, hbuf, bufs, part, square, n1, f1, n2, f2, a1, a2, a3, a4):
     cells = lin4.shape[1]
     sums = Sums({"stat": (n1, f1), "table": (n2, f2)}, (a1, a2, a3, a4))
     comes = {}
@@ -644,7 +662,42 @@
     for i in range(2):
         part[i, pl.ds(H, 96), :] = jnp.zeros((96, 128), F32)
     square[...] = jnp.zeros_like(square)
+    for buf in (upper, lower):
+        buf[pl.ds(0, 8), :] = jnp.zeros((8, 896), F32)
+        buf[pl.ds(904, 8), :] = jnp.zeros((8, 896), F32)
+    rows[pl.ds(1904, 32), :] = jnp.zeros((32, 896), F32)
     greet_all(sums.others())
+
+    def keep(r, v):
+        upper[pl.ds(r + 4, v.shape[0]), pl.ds(0, H)] = v
+        lower[pl.ds(r + 5, v.shape[0]), pl.ds(0, H)] = v
+
+    def turned(v, places):
+        lane = lax.broadcasted_iota(jnp.int32, v.shape, 1)
+        return sum(jnp.where(jnp.logical_and(lane >= to, lane < to + stop - start), pltpu.roll(v, (to - start) % 896, 1), 0.0)
+                   for start, stop, to in places)
+
+    def padded(v):
+        return jnp.concatenate([v, jnp.zeros((v.shape[0], 896 - v.shape[1]), F32)], axis=1)
+
+    def pack():
+        keep(100, gnorm[5:6, pl.ds(0, H)])
+        keep(101, gnorm[4:5, pl.ds(0, H)])
+        keep(902, gnorm[7:8, pl.ds(0, H)])
+        keep(903, gnorm[6:7, pl.ds(0, H)])
+
+        def bend(r):
+            lane = lax.broadcasted_iota(jnp.int32, (16, 896), 1)
+            rows[pl.ds(pl.multiple_of(1000 + r.start, 8), 16), :] = jnp.where(
+                lane < 200, pltpu.roll(lower[r, :], 296, 1), pltpu.roll(upper[r, :], 200, 1))
+        rows_loop(912, bend, 16, 3)
+        acc = 0.0
+        for i in range(4):
+            for j, half in enumerate((gwh, gwl)):
+                acc = acc + turned(padded(half[pl.ds(i, 200, stride=4), :]), ((0, L, 200 * i + L * j),))
+        rows[pl.ds(804, 200), :] = acc
+        rows[pl.ds(802, 1), :] = gnorm[3:4, :]
+        rows[pl.ds(803, 1), :] = gnorm[2:3, :]
 
     def norm(k, g, lin, out, between=None):
         centre, inverse = stat[2 * k:2 * k + 1, :], stat[2 * k + 1:2 * k + 2, :]
@@ -683,7 +736,7 @@
     comes["act3"].wait()
 
     def grads4():
-        gwd2[...] = mm(act3[...], dbuf[...], NT).astype(BF16)
+        keep(102, mm(act3[...], dbuf[...], NT))
     norm(2, pbuf, lin3, hbuf, grads4)
     dl = mm(wd1[...], hbuf[...], NN).astype(BF16)
     cond = mm(hot[...], dl, NT)
@@ -691,7 +744,7 @@
     low = jnp.where(lax.broadcasted_iota(jnp.int32, (4, LP), 0) == 0, sq, 0.0)
 
     def grads3():
-        gwd1[...] = mm(latent[...], hbuf[...], NT).astype(BF16)
+        keep(0, mm(latent[...], hbuf[...], NT)[:L])
     t = sums("table", jnp.concatenate([cond, low]), grads3)
     sums2[...] = t
     cond = t[0:NC, :]
@@ -706,21 +759,32 @@
         dl + change + (KL_WEIGHT / total) * mu,
         0.5 * dl * jnp.exp(0.5 * lv) * eps[...].astype(F32) + (0.5 * KL_WEIGHT / total) * (jnp.exp(lv) - 1.0)]).astype(BF16)
     dbuf[pl.ds(0, 2 * LP), :] = dh
-    gbh[...] = mm(jnp.ones((8, cells), BF16), dh, NT)
+    bias = padded(mm(jnp.ones((8, cells), BF16), dh, NT))
+    lower[pl.ds(4, 1), :] = turned(bias, ((0, L, 600), (LP, LP + L, 700)))[0:1]
     pbuf[...] = mm(wh[...], dh, NN)
     comes["lin2"].wait()
     comes["act2"].wait()
 
     def grads2():
-        gwh[...] = mm(act2[...], dbuf[pl.ds(0, 2 * LP), :], NT).astype(BF16)
+        g = mm(act2[...], dbuf[pl.ds(0, 2 * LP), :], NT)
+        gwh[...] = g[:, :LP]
+        gwl[...] = g[:, LP:]
     norm(1, pbuf, lin2, hbuf, grads2)
     pbuf[...] = mm(w2[...], hbuf[...], NN)
     comes["lin1"].wait()
     comes["act1"].wait()
 
     def grads1():
-        gw2[...] = mm(act1[...], hbuf[...], NT).astype(BF16)
+        rows[pl.ds(2, H), pl.ds(0, H)] = mm(act1[...], hbuf[...], NT)
+        pack()
     norm(0, pbuf, lin1, d1, grads1)
+    rows[pl.ds(0, 1), :] = gnorm[1:2, :]
+    rows[pl.ds(1, 1), :] = gnorm[0:1, :]
+
+    def out(r):
+        tail[r, :] = rows[r, pl.ds(0, H)].astype(BF16)
+    rows_loop(1920, out, 16, 5)
+    tail[pl.ds(1920, 16), :] = jnp.zeros((16, H), BF16)
 
 
 def hidden_backward(total, g4, lin4, w2, wh, wd1, wd2, grows, stat, latent, heads, hot, eps, table, squares, acts, lins, cid=3):
@@ -731,11 +795,10 @@
     S = jax.ShapeDtypeStruct
     return pl.pallas_call(
         functools.partial(backward_kernel, total),
-        out_shape=(S((H, cells), BF16), S((H, H), BF16), S((H, 2 * LP), BF16), S((LP, H), BF16), S((H, H), BF16),
-                   S((8, 2 * LP), F32), S((8, 896), F32), S((8, LP), F32)),
+        out_shape=(S((H, cells), BF16), S((1936, H), BF16), S((8, LP), F32)),
         in_specs=[vm] * 14 + [hbm] * 6,
-        out_specs=[vm] * 8,
-        scratch_shapes=[*[V((H, cells), BF16)] * 3, *[V((H, cells), F32)] * 3, pltpu.SemaphoreType.DMA((6,)),
+        out_specs=[vm] * 3,
+        scratch_shapes=[V((8, 896), F32), V((1936, 896), F32), V((912, 896), F32), V((912, 896), F32), V((H, LP), F32), V((H, LP), F32), *[V((H, cells), BF16)] * 3, *[V((H, cells), F32)] * 3, pltpu.SemaphoreType.DMA((6,)),
                         V((H, cells), F32), V((H, cells), BF16), V((H, cells), BF16),
                         V((4, 896, 128), F32), V((2, 896, 128), F32), V((LP, LP), F32), *sums_scratch(4, 1)],
         compiler_params=pltpu.CompilerParams(collective_id=cid, has_side_effects=True, vmem_limit_bytes=58 * 2**20),
@@ -745,19 +808,23 @@
 
 ZF, ZD = (0, 1, 2), (2, 3)
 
-def reduce_kernel(FG, DG, fo, do, tF, tD, cF, cD, rF, rD, aF, aD, bF, bD, uF, uD, vF, vD, send, recv, loc):
+def reduce_kernel(FG, DG, fo, do, nf, pd, tF, tD, cF, cD, rF, rD, aF, aD, bF, bD, uF, uD, vF, vD, send, recv, loc, hsend, hrecv):
     z, x, y, c = place()
+    XP, YP, CP = (z, 1 - x, y, c), (z, x, 1 - y, c), (z, x, y, 1 - c)
+    UP, DN = (z + 1, x, y, c), (z - 1, x, y, c)
+    me = index(z, x, y, c)
+    numbered = lambda i: (lax.shift_right_arithmetic(i, 2), lax.bitwise_and(i, 3))
+    before, after = numbered(jnp.maximum(me - 1, 0)), numbered(jnp.minimum(me + 1, 31))
+    nf[...] = jnp.zeros_like(nf)
+    pd[...] = jnp.zeros_like(pd)
     bar = pltpu.get_barrier_semaphore()
     sig = lambda d: pl.semaphore_signal(bar, inc=1, device_id=d, device_id_type=MESH)
-    XP, YP, CP = (z, 1 - x, y, c), (z, x, 1 - y, c), (z, x, y, 1 - c)
-    UP, DN = (z + 1, x, y, c), (z - 1, x, y, c)
     for d in (XP, YP, CP):
         sig(dev(*d))
-    @pl.when(z > 0)
-    def _(): sig(dev(*DN))
-    @pl.when(z < 3)
-    def _(): sig(dev(*UP))
-    pl.semaphore_wait(bar, 3 + (z > 0).astype(jnp.int32) + (z < 3).astype(jnp.int32))
+    for cond, d in ((z > 0, dev(*DN)), (z < 3, dev(*UP)), (me > 0, before), (me < 31, after)):
+        pl.when(cond)(functools.partial(sig, d))
+    one = lambda cond: cond.astype(jnp.int32)
+    pl.semaphore_wait(bar, 3 + one(z > 0) + one(z < 3) + one(me > 0) + one(me < 31))
 
     sems = {}
     def sem_index(key):
@@ -765,14 +832,13 @@
     started = []
 
     def cases(s, part):
-        e = d_unit(s)
-        four = jnp.logical_and(s >= NF, (d_unit(s + 1) - e) == 4)
+        last = jnp.logical_and(s >= NF, four(s))
         f, d = s < NF, s >= NF
         if part == "all":
-            return [(f, "F", 0, 496, 0), (d, "D", 0, 48, 0), (four, "D", 48, 16, 1)]
+            return [(f, "F", 0, 496, 0), (d, "D", 0, 48, 0), (last, "D", 48, 16, 1)]
         if part == "a":
             return [(f, "F", 0, 240, 0), (d, "D", 0, 32, 0)]
-        return [(f, "F", 240, 256, 0), (d, "D", 32, 16, 0), (four, "D", 48, 16, 1)]
+        return [(f, "F", 240, 256, 0), (d, "D", 32, 16, 0), (last, "D", 48, 16, 1)]
 
     def land(pair, zz, b, col=None):
         buf = pair[0 if b == "F" else 1]
@@ -909,7 +975,6 @@
             total(s, guard, "all", zz, on(C, 0), base)
         go(guard, s, zz, "all", (name, t), to, on(C, 0), on(pair))
 
-    me = index(z, x, y, c)
     @pl.when(me >= NF)
     def _(): fo[...] = jnp.zeros_like(fo)
     do[pl.ds(48, 16), :] = jnp.zeros((16, 7000), jnp.float32)
@@ -924,9 +989,22 @@
             second(i - 1)
         if i >= 2:
             third(i - 2)
+    edge = lambda k, src, dst, to: pltpu.make_async_remote_copy(
+        src_ref=src, dst_ref=dst, send_sem=hsend.at[k], recv_sem=hrecv.at[k], device_id=to, device_id_type=MESH)
+    edges = [(jnp.logical_and(me >= 1, me < NF), me < NF - 1, edge(0, fo.at[pl.ds(0, 32)], nf, before)),
+             (me == NF, me == NF - 1, edge(2, do.at[pl.ds(0, 16)], pd, before))]
+    inner = jnp.logical_and(me >= NF, me < 31)
+    edges += [(jnp.logical_and(inner, four(me)), jnp.logical_and(me > NF, four(me - 1)), edge(1, do.at[pl.ds(48, 16)], pd, after)),
+              (jnp.logical_and(inner, jnp.logical_not(four(me))), jnp.logical_and(me > NF, jnp.logical_not(four(me - 1))),
+               edge(1, do.at[pl.ds(32, 16)], pd, after))]
+    for out, _, cp in edges:
+        pl.when(out)(cp.start)
     for guard, a in started:
         for cond, cp in make(*a):
             grd(cond, guard, cp.wait_send)
+    for out, into, cp in edges:
+        pl.when(out)(cp.wait_send)
+        pl.when(into)(cp.wait_recv)
 
 def reduce(FG, DG, cid=2):
     B16 = jnp.bfloat16
@@ -934,29 +1012,24 @@
     pair = lambda *lead: [V(lead + (3, FROWS, 800), B16), V(lead + (2, DROWS, 7000), B16)]
     return pl.pallas_call(
         reduce_kernel,
-        out_shape=(jax.ShapeDtypeStruct((FROWS, 800), jnp.float32), jax.ShapeDtypeStruct((DROWS, 7000), jnp.float32)),
+        out_shape=(jax.ShapeDtypeStruct((FROWS, 800), jnp.float32), jax.ShapeDtypeStruct((DROWS, 7000), jnp.float32),
+                   jax.ShapeDtypeStruct((32, 800), jnp.float32), jax.ShapeDtypeStruct((16, 7000), jnp.float32)),
         in_specs=[pl.BlockSpec(memory_space=pl.ANY)] * 2,
-        out_specs=[pl.BlockSpec(memory_space=V)] * 2,
+        out_specs=[pl.BlockSpec(memory_space=V)] * 4,
         scratch_shapes=[V((2, FROWS, 800), B16), V((2, DROWS, 7000), B16), *pair(4), *pair(2), *pair(), *pair(), *pair(), *pair(),
-                        pltpu.SemaphoreType.DMA((192,)), pltpu.SemaphoreType.DMA((192,)), pltpu.SemaphoreType.DMA((2, 2))],
+                        pltpu.SemaphoreType.DMA((192,)), pltpu.SemaphoreType.DMA((192,)), pltpu.SemaphoreType.DMA((2, 2)),
+                        pltpu.SemaphoreType.DMA((3,)), pltpu.SemaphoreType.DMA((3,))],
         compiler_params=pltpu.CompilerParams(collective_id=cid, has_side_effects=True, vmem_limit_bytes=60 * 2**20),
         name="sum_gradients",
     )(FG, DG)
 
-def flatten(fo, do):
-    n = 32
+def flatten(fo, do, nf, pd):
     me = lax.axis_index("wide") * 4 + lax.axis_index("narrow")
-    ax = ("wide", "narrow")
-    nextf = lax.ppermute(fo[:26], ax, [(i + 1, i) for i in range(n - 1)]).reshape(-1)
-    nextd = lax.ppermute(do[:6], ax, [(18, 17)]).reshape(-1)
-    e = d_unit(me)
-    last = 16 * jnp.maximum(d_unit(me + 1) - e - 1, 0)
-    prevd = lax.ppermute(lax.dynamic_slice(do, (last, 0), (16, 7000)), ax, [(i, i + 1) for i in range(n - 1)]).reshape(-1)
-    ff = fo.reshape(-1)
+    ff, nextf, edge = fo.reshape(-1), nf.reshape(-1)[:20800], pd.reshape(-1)
     a = lax.dynamic_slice(jnp.concatenate([ff, nextf]), (1152 * jnp.minimum(me, 16),), (SHARD,))
-    b = jnp.concatenate([ff[19584:381000], nextd[:36536]])
-    off = 112000 - (112000 * e + 7126600 - SHARD * me)
-    c = lax.dynamic_slice(jnp.concatenate([prevd, do.reshape(-1)]), (jnp.clip(off, 0, 560000 - SHARD),), (SHARD,))
+    b = jnp.concatenate([ff[19584:381000], edge[:36536]])
+    off = 112000 - (112000 * d_unit(me) + FLATF - SHARD * me)
+    c = lax.dynamic_slice(jnp.concatenate([edge, do.reshape(-1)]), (jnp.clip(off, 0, 560000 - SHARD),), (SHARD,))
     return jnp.where(me < 17, a, jnp.where(me == 17, b, c))
 
 
@@ -1017,10 +1090,6 @@
     wide = [(0, 0)] * a.ndim
     wide[axis] = (0, LP - L)
     return jnp.concatenate([jnp.pad(lax.slice_in_dim(a, i, i + L, axis=axis), wide) for i in (0, L)], axis=axis)
-
-
-def unhalved(a, axis):
-    return jnp.concatenate([lax.slice_in_dim(a, i, i + L, axis=axis) for i in (0, LP)], axis=axis)
 
 
 def one_hot(labels):
@@ -1045,13 +1114,11 @@
     offset = cond_sums / counts[:, None] - jnp.sum(cond_sums, axis=0) / total
     mask_total = jnp.sum(counts * jnp.sum(panels.astype(F32), axis=1))
     rebuilt, direct, DG, g4, squares = output_layer(D, ends, x, panels.astype(BF16), hot, 2.0 / mask_total)
-    d1, gw2, gwh, gwd1, gwd2, gbh, gnorm, sums2 = hidden_backward(
+    d1, tail, sums2 = hidden_backward(
         total, g4, lin4, w[3], wh, wd1, w[11], grows, stat, latent, heads, hot, eps, table, squares,
         (act1, act2, act3), (lin1, lin2, lin3))
     FG, grad_cells = last_layer(x, F, d1, direct, FROWS * NF)
-    gn = gnorm[:, :H]
-    tail = pack_rows([gn[1], gn[0], gw2, gn[3], gn[2], unhalved(gwh, 1), unhalved(gbh[0], 0), gwd1[:L], gn[5], gn[4], gwd2, gn[7], gn[6]])
-    FG = lax.dynamic_update_slice(FG, tail, (G, 0))
+    FG = lax.dynamic_update_slice(FG, tail[:FROWS * NF - G], (G, 0))
     grad_params = flatten(*reduce(FG, DG, 4))
     divergence = -0.5 * table[NC, 0] / total
     loss = sums2[NC, 0] / mask_total + KL_WEIGHT * divergence

time: 638 us -> 599 us (0.939)
  local copies, waits for them, and re-layouts: 67.9 us -> 34.9 us
  Pallas kernels: 514 us -> 526 us
  starting transfers between devices: 15.5 us -> 5.63 us
    concatenate x2 -> x0, local copies, waits for them, and re-layouts: 24.9 us -> none  [the longest x1 16.4 us: pack_rows(): jnp.concatenate([row(g[0]), row(g[1]), g[2], row(g[3]), row(g[4]), g[5].r...]
    pallas_call x1, Pallas kernels: 137 us -> 149 us  [reduce(): pl.pallas_call(reduce_kernel, out_shape=(jax.ShapeDtypeStruct((FROWS, 800...]
    ppermute x3 -> x0, starting transfers between devices: 9.9 us -> none  [the longest x1 6.09 us: flatten(): lax.ppermute(lax.dynamic_slice(do, (last, 0), (16, 7000)), ax, [(i, i + 1...]
  transfers between devices with their start and end apart: 5 -> 2, of which waited for: 1 -> 0; matrix products, arithmetic and copies ran while one was open for 2% -> 1% of each run, Pallas kernels for 0% -> 0%
where the time goes in v2:
time: 599 us; the launch traced here: 589 us
  Pallas kernels  526 us (88%)
  local copies, waits for them, and re-layouts  34.9 us (6%)
  other arithmetic  15.8 us (3%)
  between operations  6.88 us (1%)
    pallas_call x1, Pallas kernels, reduce(): pl.pallas_call(reduce_kernel, out_shape=(jax.ShapeDtypeStruct((FROWS, 800...  149 us
    pallas_call x1, Pallas kernels, spread_and_first(): pl.pallas_call(first_kernel, out_shape=(jax.ShapeDtypeStruct((FROWS * NF,...  147 us
    pallas_call x1, Pallas kernels, hidden_backward(): pl.pallas_call(functools.partial(backward_kernel, total), out_shape=(S((H...  66.3 us
    pallas_call x1, Pallas kernels, output_layer(): pl.pallas_call(functools.partial(output_kernel, part, block), grid=(n,),...  65.4 us
    pallas_call x1, Pallas kernels, hidden_layers(): pl.pallas_call(functools.partial(forward_kernel, total), out_shape=(S((H,...  59.8 us
    pallas_call x1, Pallas kernels, last_layer(): pl.pallas_call(last_kernel, grid=(pl.cdiv(G, block),), out_shape=(jax.Sha...  38.2 us
  transfers between devices with their start and end apart: 2, of which 0 were waited for; matrix products, arithmetic and copies ran while one was open for 1% of the time, Pallas kernels for 0%

profile of v2, /device:TPU:17, one launch (start us, length us, event | category | flops | bytes accessed | tf_op | source)
XLA Modules:
  0.0 589.4 jit_solution(4578972982736314645)
XLA Ops:
  1.7 2.6 collective-permute-start.1
  5.2 3.0 collective-permute-start
  8.2 1.3 fusion.9.hot.h_ref
  9.5 1.5 convert_element_type.44.p_ref
  11.1 1.7 pad.38.eps
  14.5 2.3 reshape.50.ds
  17.3 2.2 reshape.49.fs
  19.5 147.3 %spread_and_first.1 = (bf16[8928,800]{1,0:T(8,128)(2,1)}, bf16[816,7000]{1,0:T(8,128)(2,1)}, f32[800,1024]{1,0:T(8,128)}) custom-call(bf16[496,800]{1,0:T(8,128)(2,1)} %reshape.49.fs, bf16[7000,1024]{1,0:T(8,128)(2,1)} %bitcast.14, bf16[64,7000]{1,0:T(8,128)(2,1)} %reshape.50.ds), custom_call_target="tpu_custom_call" | custom-call | tf_op jit(solution)/shard_map/spread_and_first/pallas_call | solution.py:431
  166.8 2.3 slice.99
  171.0 1.7 fusion.4.wd2
  175.8 2.8 slice.95.w2
  181.1 59.8 %hidden_layers.1 = (bf16[800,1024]{1,0:T(8,128)(2,1)}, bf16[800,1024]{1,0:T(8,128)(2,1)}, bf16[800,1024]{1,0:T(8,128)(2,1)}, bf16[816,1024]{1,0:T(8,128)(2,1)}, ...) custom-call(f32[800,1024]{1,0:T(8,128)} %get-tuple-element.34.lin1.l, ...), custom_call_target="tpu_custom_call" | custom-call | tf_op jit(solution)/shard_map/hidden_layers/pallas_call | solution.py:639
  241.8 1.2 slice.114
  244.9 65.4 %output_layer.1 = (bf16[7000,1024]{1,0:T(8,128)(2,1)}, bf16[7000,1024]{1,0:T(8,128)(2,1)}, bf16[816,7000]{1,0:T(8,128)(2,1)}, f32[816,1024]{1,0:T(8,128)}, f32[8,1024]{1,0:T(8,128)}) custom-call(f32[1]{0:T(128)} %bitcast.5.scale, bf16[816,7000]{1,0:T(8,128)(2,1)} %get-tuple-element.37.d_ref, bf16[816,1024]{1,0:T(8,128)(2,1)} %get-tuple-element.38.a_ref, ...), custom_call_target="tpu_custom_call" | custom-call | flops 34406400000 | bytes 70000000 | tf_op jit(solution)/shard_map/output_layer/pallas_call | solution.py:65
  310.3 66.3 %hidden_backward.1 = (bf16[800,1024]{1,0:T(8,128)(2,1)}, bf16[1936,800]{1,0:T(8,128)(2,1)}, f32[8,128]{1,0:T(8,128)}) custom-call(f32[816,1024]{1,0:T(8,128)} %get-tuple-element.40.g4, f32[800,1024]{1,0:T(8,128)} %get-tuple-element.41.lin4, bf16[800,800]{1,0:T(8,128)(2,1)} %slice.95.w2, bf16[800,256]{1,0:T(8,128)(2,1)} %fusion.6.wh, ...), custom_call_target="tpu_custom_call" | custom-call | tf_op jit(solution)/shard_map/hidden_backward/pallas_call | solution.py:796
  376.6 38.2 %last_layer.1 = (bf16[8928,800]{1,0:T(8,128)(2,1)}, bf16[7000,1024]{1,0:T(8,128)(2,1)}) custom-call(bf16[7000,1024]{1,0:T(8,128)(2,1)} %bitcast.16, bf16[8928,800]{1,0:T(8,128)(2,1)} %get-tuple-element.35.w_ref, bf16[800,1024]{1,0:T(8,128)(2,1)} %get-tuple-element.52.d_ref, bf16[7000,1024]{1,0:T(8,128)(2,1)} %get-tuple-element.53.t_ref), custom_call_target="tpu_custom_call" | custom-call | flops 22937600000 | bytes 70000000 | tf_op jit(solution)/shard_map/last_layer/pallas_call | solution.py:122
  414.8 2.1 slice_dynamic-update-slice_fusion.FG
  416.8 149.4 %sum_gradients.1 = (f32[496,800]{1,0:T(8,128)}, f32[64,7000]{1,0:T(8,128)}, f32[32,800]{1,0:T(8,128)}, f32[16,7000]{1,0:T(8,128)}) custom-call(bf16[8928,800]{1,0:T(8,128)(2,1)} %slice_dynamic-update-slice_fusion.FG, bf16[816,7000]{1,0:T(8,128)(2,1)} %get-tuple-element.57.DG), custom_call_target="tpu_custom_call" | custom-call | tf_op jit(solution)/shard_map/sum_gradients/pallas_call | solution.py:1013
  566.2 2.6 reshape.53
  568.8 1.2 slice.128
  570.0 2.7 reshape.55
  572.7 2.0 reshape.54
  575.7 1.6 slice.117
  581.9 4.8 fusion.1
  (42 shorter events, 16.6 us)
Async XLA Ops:
  0.6 13.2 %copy-start.1 = (bf16[397952]{0:T(1024)(128)(2,1)S(1)}, bf16[397952]{0:T(1024)(128)(2,1)}, u32[]{:S(2)}) copy-start(bf16[397952]{0:T(1024)(128)(2,1)} %param.7) | copy-start | bytes 2387716
  1.7 12.1 %collective-permute-start.1 = (bf16[112000]{0:T(1024)(128)(2,1)S(1)}, bf16[112000]{0:T(1024)(128)(2,1)S(1)}, u32[]{:S(2)}, u32[]{:S(2)}) collective-permute-start(bf16[112000]{0:T(1024)(128)(2,1)S(1)} %slice.94), channel_id=1, source_target_pairs={{1,0},{2,1},{3,2},{4,3},{5,4},{6,5},{7,6},{8,7},{9,8},{10,9},{11,1... | collective-permute-start | bytes 672008 | tf_op jit(solution)/shard_map/ppermute | solution.py:449
  5.2 8.6 %collective-permute-start = (bf16[36864]{0:T(1024)(128)(2,1)S(1)}, bf16[36864]{0:T(1024)(128)(2,1)S(1)}, u32[]{:S(2)}, u32[]{:S(2)}) collective-permute-start(bf16[36864]{0:T(1024)(128)(2,1)S(1)} %slice.93), channel_id=1, source_target_pairs={{0,1},{1,2},{2,3},{3,4},{4,5},{5,6},{6,7},{7,8},{8,9},{9,10},{10,1... | collective-permute-start | bytes 221192 | tf_op jit(solution)/shard_map/ppermute | solution.py:448
  171.0 2.8 copy-start.3
  175.8 3.6 copy-start.4
  376.6 38.2 %copy-start = (bf16[1936,800]{1,0:T(8,128)(2,1)S(1)}, bf16[1936,800]{1,0:T(8,128)(2,1)}, u32[]{:S(2)}) copy-start(bf16[1936,800]{1,0:T(8,128)(2,1)} %get-tuple-element.56) | copy-start | bytes 9292804
  570.0 9.8 %copy-start.2 = (f32[8,128]{1,0:T(8,128)S(1)}, f32[8,128]{1,0:T(8,128)}, u32[]{:S(2)}) copy-start(f32[8,128]{1,0:T(8,128)} %get-tuple-element.36.table) | copy-start | bytes 12292

commit v3 on v2

--- a/solution.py
+++ b/solution.py
@@ -185,6 +185,9 @@
 
 
 class Spread:
+    VIA = {"F": (None, (0b0111, 0b0111), (0b0010, 0b0101), (0b0000, 0b0001)),
+           "D": (None, (0b1100, 0b1100), (0b1000, 0b1100), (0b1000, 0b0000))}
+
     def __init__(self, kind, own, buf, send, recv, base=0):
         self.kind, self.own, self.buf, self.send, self.recv = kind, own, buf, send, recv
         self.place = z, x, y, c = place()
@@ -281,12 +284,17 @@
                         f((p,))
             self.where(s, ok, fn)
 
+    def by_z(self, t, zz):
+        first, others = self.VIA[self.kind][t]
+        has = lambda planes: lax.bitwise_and(lax.shift_right_arithmetic(planes, jnp.clip(zz, 0, 3)), 1) == 1
+        return has(first), has(others)
+
     def flat_parts(self, tag):
         _, zz, guard = self.tags[tag]
         if tag == 0:
-            return (guard, guard)
-        even = lax.rem(zz + 4, 2) == 0
-        return jnp.logical_and(guard, even), jnp.logical_and(guard, jnp.logical_not(even))
+            return guard, guard
+        first, others = self.by_z(tag // 2, zz)
+        return jnp.logical_and(guard, jnp.logical_not(others)), jnp.logical_and(guard, jnp.logical_not(first))
 
     def cross(self, tag):
         _, zz, guard = self.tags[tag]
@@ -312,15 +320,14 @@
         both = lambda a, b: b if a is None else jnp.logical_and(a, b)
         gets, legs = [], []
         if tag:
-            frm, to, more = (self.DN, self.UP, z < 3) if name == "u" else (self.UP, self.DN, z > 0)
-            gets = [self.gets(sd, (0,), ("g" + name, t), frm, second), self.gets(sd, (1, 2), ("g" + name, t), frm, half)]
-            if t < 3:
-                legs = [((0,), ("g" + name, t + 1), to, both(second, more)), ((1, 2), ("g" + name, t + 1), to, both(half, more))]
-        else:
-            even = lax.rem(z, 2) == 0
-            odd = jnp.logical_not(even)
-            for name, to, more in (("u", self.UP, z < 3), ("d", self.DN, z > 0)):
-                legs += [((0,), ("g" + name, 1), to, both(even, more)), ((1, 2), ("g" + name, 1), to, both(odd, more))]
+            frm = self.DN if name == "u" else self.UP
+            first, others = self.by_z(t, zz)
+            gets = [self.gets(sd, (0,), ("g" + name, t), frm, both(guard, first)),
+                    self.gets(sd, (1, 2), ("g" + name, t), frm, both(guard, others))]
+        for name in ("ud"[tag % 2] if tag else "ud") if t < 3 else "":
+            to, more = (self.UP, z < 3) if name == "u" else (self.DN, z > 0)
+            first, others = self.by_z(t + 1, zz)
+            legs += [((0,), ("g" + name, t + 1), to, both(first, more)), ((1, 2), ("g" + name, t + 1), to, both(others, more))]
         gets += [self.gets(sd, (1, 2), ("xy", tag), self.YP, second), self.gets(sd, (0,), ("yx", tag), self.XP, half)]
         send = self.sends(sd, guard, legs + [(ALL, ("c3", tag), self.CP, None)])
 
@@ -433,9 +440,9 @@
         out_shape=(jax.ShapeDtypeStruct((FROWS * NF, H), BF16), jax.ShapeDtypeStruct((HX, G), BF16), jax.ShapeDtypeStruct((H, cells), F32)),
         in_specs=[pl.BlockSpec(memory_space=pl.ANY)] * 3,
         out_specs=[pl.BlockSpec(memory_space=pl.ANY)] * 2 + [pl.BlockSpec(memory_space=V)],
-        scratch_shapes=[V((FROWS * NF, H), BF16), V((G, cells), BF16), pltpu.SemaphoreType.DMA((128,)), pltpu.SemaphoreType.DMA((128,)),
+        scratch_shapes=[V((FROWS * NF, H), BF16), V((G, cells), BF16), pltpu.SemaphoreType.DMA((144,)), pltpu.SemaphoreType.DMA((144,)),
                         pltpu.SemaphoreType.DMA((3,)), pltpu.SemaphoreType.DMA((64,)), pltpu.SemaphoreType.DMA,
-                        pltpu.SemaphoreType.DMA((192,)), pltpu.SemaphoreType.DMA((192,)), pltpu.SemaphoreType.DMA((3,))],
+                        pltpu.SemaphoreType.DMA((208,)), pltpu.SemaphoreType.DMA((208,)), pltpu.SemaphoreType.DMA((3,))],
         compiler_params=pltpu.CompilerParams(collective_id=cid, has_side_effects=True, vmem_limit_bytes=58 * 2**20),
         name="spread_and_first",
     )(fslot, x, dslot)
@@ -544,12 +551,24 @@
             dma((n, 8)), dma((n, 8)), dma((n, 4)), dma((n, 4))]
 
 
-def forward_kernel(total, lin1, w2, wh, wd1, wd2, grows, bh, hot, eps,
+def turned(v, places):
+    lane = lax.broadcasted_iota(jnp.int32, v.shape, 1)
+    return sum(jnp.where(jnp.logical_and(lane >= to, lane < to + stop - start), pltpu.roll(v, (to - start) % 896, 1), 0.0)
+               for start, stop, to in places)
+
+
+def padded(v):
+    return jnp.concatenate([v, jnp.zeros((v.shape[0], 896 - v.shape[1]), F32)], axis=1)
+
+
+def forward_kernel(total, lin1, F, hot, eps, w2, wh, wd1, wd2, grows,
                    act1o, act2o, act3o, ends, heads, latent, lin2o, lin3o, lin4, stat, table,
-                   act1, act2, act3, lin2, lin3, osem, bufs, square, n1, f1, n2, f2, a1, a2, a3, a4):
+                   packed, msem, rows, tail, whm, whl, bh, act1, act2, act3, lin2, lin3, osem, bufs, square, n1, f1, n2, f2, a1, a2, a3, a4):
     z, x, y, c = place()
     sums = Sums({"stat": (n1, f1), "table": (n2, f2)}, (a1, a2, a3, a4))
     cells = lin1.shape[1]
+    brings = pltpu.make_async_copy(F.at[pl.ds(6992, 1920)], packed, msem)
+    brings.start()
     for i in range(2):
         bufs[i, pl.ds(H, 96), :] = jnp.zeros((96, 128), F32)
     square[...] = jnp.zeros_like(square)
@@ -577,6 +596,30 @@
             out[r, :] = silu(lin[r, :] * wide(bufs[0, r, :], cells) + wide(bufs[1, r, :], cells)).astype(BF16)
         rows_loop(H, one)
 
+    def unpack():
+        brings.wait()
+
+        def widen(r):
+            rows[r, :] = padded(packed[r, :].astype(F32))
+        rows_loop(1920, widen, 32, 5)
+        lane = lax.broadcasted_iota(jnp.int32, (904, 896), 1)
+        t = jnp.where(lane < 600, pltpu.roll(rows[pl.ds(1012, 904), :], 696, 1), pltpu.roll(rows[pl.ds(1013, 904), :], 600, 1))
+        tail[...] = jnp.where(lane < H, t, 0.0)
+        for i, (buf, r) in enumerate(((rows, 8), (rows, 9), (rows, 810), (rows, 811), (tail, 100), (tail, 101), (tail, 902), (tail, 903))):
+            grows[pl.ds(i, 1), :] = buf[pl.ds(r, 1), :]
+        w2[...] = rows[pl.ds(10, H), pl.ds(0, H)].astype(BF16)
+        wd2[...] = tail[pl.ds(102, H), pl.ds(0, H)].astype(BF16)
+        top = lax.broadcasted_iota(jnp.int32, (LP, H), 0) < L
+        wd1[...] = jnp.where(top, tail[pl.ds(0, LP), pl.ds(0, H)], 0.0).astype(BF16)
+        v = rows[pl.ds(812, 200), :]
+        for i in range(4):
+            for k, half in enumerate((whm, whl)):
+                half[pl.ds(i, 200, stride=4), :] = turned(v, ((200 * i + L * k, 200 * i + L * k + L, 0),))[:, :LP]
+        wh[:, pl.ds(0, LP)] = whm[...].astype(BF16)
+        wh[:, pl.ds(LP, LP)] = whl[...].astype(BF16)
+        b = turned(rows[pl.ds(1012, 1), :], ((0, L, 0), (L, 2 * L, LP)))[:, :2 * LP]
+        bh[...] = jnp.transpose(jnp.broadcast_to(b, (LP, 2 * LP)))
+
     leaving = []
 
     def leave(src, dst):
@@ -584,13 +627,13 @@
         cp.start()
         leaving.append(cp)
 
-    norm(0, lin1, act1)
+    norm(0, lin1, act1, unpack)
     lin2[...] = mm(w2[...], act1[...], TN)
     leave(act1, act1o)
     leave(lin2, lin2o)
     norm(1, lin2, act2)
     leave(act2, act2o)
-    h = (mm(wh[...], act2[...], TN) + bh[...]).astype(BF16)
+    h = (mm(wh[...], act2[...], TN) + bh[:, 0:1]).astype(BF16)
     heads[...] = h
     mu, lv = h[:LP].astype(F32), h[LP:].astype(F32)
     part = mm(hot[...], h[:LP], NT)
@@ -630,7 +673,7 @@
     pl.semaphore_wait(bar, len(devices))
 
 
-def hidden_layers(total, lin1, w2, wh, wd1, wd2, grows, bh, hot, eps, cid=2):
+def hidden_layers(total, lin1, F, hot, eps, cid=2):
     cells = lin1.shape[1]
     V = pltpu.VMEM
     vm = pl.BlockSpec(memory_space=V)
@@ -638,15 +681,17 @@
     S = jax.ShapeDtypeStruct
     return pl.pallas_call(
         functools.partial(forward_kernel, total),
-        out_shape=(S((H, cells), BF16), S((H, cells), BF16), S((H, cells), BF16), S((HX, cells), BF16), S((2 * LP, cells), BF16),
+        out_shape=(S((H, H), BF16), S((H, 2 * LP), BF16), S((LP, H), BF16), S((H, H), BF16), S((8, 896), F32),
+                   S((H, cells), BF16), S((H, cells), BF16), S((H, cells), BF16), S((HX, cells), BF16), S((2 * LP, cells), BF16),
                    S((LP, cells), BF16), S((H, cells), F32), S((H, cells), F32), S((H, cells), F32), S((8, 896), F32),
                    S((8, LP), F32)),
-        in_specs=[vm] * 9,
-        out_specs=[hbm] * 3 + [vm] * 3 + [hbm] * 2 + [vm] * 3,
-        scratch_shapes=[*[V((H, cells), BF16)] * 3, *[V((H, cells), F32)] * 2, pltpu.SemaphoreType.DMA((8,)), V((2, 896, 128), F32), V((LP, LP), F32), *sums_scratch(4, 1)],
+        in_specs=[vm, hbm, vm, vm],
+        out_specs=[vm] * 5 + [hbm] * 3 + [vm] * 3 + [hbm] * 2 + [vm] * 3,
+        scratch_shapes=[V((1920, H), BF16), pltpu.SemaphoreType.DMA, V((1920, 896), F32), V((904, 896), F32), V((H, LP), F32), V((H, LP), F32),
+                        V((2 * LP, LP), F32), *[V((H, cells), BF16)] * 3, *[V((H, cells), F32)] * 2, pltpu.SemaphoreType.DMA((8,)), V((2, 896, 128), F32), V((LP, LP), F32), *sums_scratch(4, 1)],
         compiler_params=pltpu.CompilerParams(collective_id=cid, has_side_effects=True, vmem_limit_bytes=58 * 2**20),
         name="hidden_layers",
-    )(lin1, w2, wh, wd1, wd2, grows, bh, hot, eps)
+    )(lin1, F, hot, eps)
 
 
 def backward_kernel(total, g4, lin4, w2, wh, wd1, wd2, grows, stat, latent, heads, hot, eps, table, squares, act1i, act2i, act3i, lin1i, lin2i, lin3i,
@@ -671,14 +716,6 @@
     def keep(r, v):
         upper[pl.ds(r + 4, v.shape[0]), pl.ds(0, H)] = v
         lower[pl.ds(r + 5, v.shape[0]), pl.ds(0, H)] = v
-
-    def turned(v, places):
-        lane = lax.broadcasted_iota(jnp.int32, v.shape, 1)
-        return sum(jnp.where(jnp.logical_and(lane >= to, lane < to + stop - start), pltpu.roll(v, (to - start) % 896, 1), 0.0)
-                   for start, stop, to in places)
-
-    def padded(v):
-        return jnp.concatenate([v, jnp.zeros((v.shape[0], 896 - v.shape[1]), F32)], axis=1)
 
     def pack():
         keep(100, gnorm[5:6, pl.ds(0, H)])
@@ -1086,12 +1123,6 @@
                             jnp.zeros((FROWS * NF - 8909, 800), BF16)])
 
 
-def by_halves(a, axis):
-    wide = [(0, 0)] * a.ndim
-    wide[axis] = (0, LP - L)
-    return jnp.concatenate([jnp.pad(lax.slice_in_dim(a, i, i + L, axis=axis), wide) for i in (0, L)], axis=axis)
-
-
 def one_hot(labels):
     return (labels[None, :] == jnp.arange(NC, dtype=jnp.int32)[:, None]).astype(BF16)
 
@@ -1101,21 +1132,16 @@
     x = expression.T
     hot = one_hot(labels)
     F, D, lin1 = spread_and_first(*slots(params), x)
-    w = unpack_rows(F)
     eps = jnp.pad(epsilon.T, ((0, LP - L), (0, 0)))
-    wh = by_halves(w[6], 1)
-    bh = by_halves(w[7].astype(F32), 0)[:, None]
-    wd1 = jnp.pad(w[8], ((0, LP - L), (0, 0)))
-    grows = jnp.pad(jnp.stack([w[i].astype(F32) for i in (1, 2, 4, 5, 9, 10, 12, 13)]), ((0, 0), (0, 896 - H)))
-    act1, act2, act3, ends, heads, latent, lin2, lin3, lin4, stat, table = hidden_layers(
-        total, lin1, w[3], wh, wd1, w[11], grows, bh, hot, eps)
+    w2, wh, wd1, wd2, grows, act1, act2, act3, ends, heads, latent, lin2, lin3, lin4, stat, table = hidden_layers(
+        total, lin1, F, hot, eps)
     counts = table[:NC, LP - 1]
     cond_sums = table[:NC, :L]
     offset = cond_sums / counts[:, None] - jnp.sum(cond_sums, axis=0) / total
     mask_total = jnp.sum(counts * jnp.sum(panels.astype(F32), axis=1))
     rebuilt, direct, DG, g4, squares = output_layer(D, ends, x, panels.astype(BF16), hot, 2.0 / mask_total)
     d1, tail, sums2 = hidden_backward(
-        total, g4, lin4, w[3], wh, wd1, w[11], grows, stat, latent, heads, hot, eps, table, squares,
+        total, g4, lin4, w2, wh, wd1, wd2, grows, stat, latent, heads, hot, eps, table, squares,
         (act1, act2, act3), (lin1, lin2, lin3))
     FG, grad_cells = last_layer(x, F, d1, direct, FROWS * NF)
     FG = lax.dynamic_update_slice(FG, tail[:FROWS * NF - G], (G, 0))

time: 599 us -> 570 us (0.952)
  Pallas kernels: 526 us -> 512 us
  local copies, waits for them, and re-layouts: 34.9 us -> 26.2 us
    pallas_call x1, Pallas kernels: 147 us -> 136 us  [spread_and_first(): pl.pallas_call(first_kernel, out_shape=(jax.ShapeDtypeStruct((FROWS * NF,...]
    slice x6 -> x0, local copies, waits for them, and re-layouts: 7.47 us -> none  [the longest x2 3.39 us: unpack_rows(): tail = jnp.concatenate([F[8004:8908, 200:], F[8005:8909, :200]], axis=1)]
where the time goes in v3:
time: 570 us; the launch traced here: 561 us
  Pallas kernels  512 us (90%)
  local copies, waits for them, and re-layouts  26.2 us (5%)
  other arithmetic  10.2 us (2%)
  between operations  6.58 us (1%)
    pallas_call x1, Pallas kernels, reduce(): pl.pallas_call(reduce_kernel, out_shape=(jax.ShapeDtypeStruct((FROWS, 800...  149 us
    pallas_call x1, Pallas kernels, spread_and_first(): pl.pallas_call(first_kernel, out_shape=(jax.ShapeDtypeStruct((FROWS * NF,...  136 us
    pallas_call x1, Pallas kernels, hidden_backward(): pl.pallas_call(functools.partial(backward_kernel, total), out_shape=(S((H...  66.2 us
    pallas_call x1, Pallas kernels, output_layer(): pl.pallas_call(functools.partial(output_kernel, part, block), grid=(n,),...  65.1 us
    pallas_call x1, Pallas kernels, hidden_layers(): pl.pallas_call(functools.partial(forward_kernel, total), out_shape=(S((H,...  57.9 us
    pallas_call x1, Pallas kernels, last_layer(): pl.pallas_call(last_kernel, grid=(pl.cdiv(G, block),), out_shape=(jax.Sha...  38.4 us
  transfers between devices with their start and end apart: 2, of which 0 were waited for; matrix products, arithmetic and copies ran while one was open for 1% of the time, Pallas kernels for 0%

profile of v3, /device:TPU:17, one launch (start us, length us, event | category | flops | bytes accessed | tf_op | source)
XLA Modules:
  0.0 560.5 jit_solution(15245098261314190134)
XLA Ops:
  0.6 1.0 slice.34
  1.7 2.6 collective-permute-start.1
  5.2 3.0 collective-permute-start
  8.2 1.3 fusion.4.hot.h_ref
  9.5 1.5 convert_element_type.13.p_ref
  11.0 1.7 pad.4.eps
  12.7 1.1 convert_reduce_fusion
  14.5 2.3 reshape.41.ds
  17.3 2.2 reshape.40.fs
  19.5 135.7 %spread_and_first.1 = (bf16[8928,800]{1,0:T(8,128)(2,1)}, bf16[816,7000]{1,0:T(8,128)(2,1)}, f32[800,1024]{1,0:T(8,128)}) custom-call(bf16[496,800]{1,0:T(8,128)(2,1)} %reshape.40.fs, bf16[7000,1024]{1,0:T(8,128)(2,1)} %bitcast.9, bf16[64,7000]{1,0:T(8,128)(2,1)} %reshape.41.ds), custom_call_target="tpu_custom_call" | custom-call | tf_op jit(solution)/shard_map/spread_and_first/pallas_call | solution.py:438
  155.2 57.9 %hidden_layers.1 = (bf16[800,800]{1,0:T(8,128)(2,1)}, bf16[800,256]{1,0:T(8,128)(2,1)}, bf16[128,800]{1,0:T(8,128)(2,1)}, bf16[800,800]{1,0:T(8,128)(2,1)}, f32[...) custom-call(f32[800,1024]{1,0:T(8,128)} %get-tuple-element.39.lin1.l, ...), custom_call_target="tpu_custom_call" | custom-call | tf_op jit(solution)/shard_map/hidden_layers/pallas_call | solution.py:682
  214.0 1.2 slice.38
  217.2 65.1 %output_layer.1 = (bf16[7000,1024]{1,0:T(8,128)(2,1)}, bf16[7000,1024]{1,0:T(8,128)(2,1)}, bf16[816,7000]{1,0:T(8,128)(2,1)}, f32[816,1024]{1,0:T(8,128)}, f32[8,1024]{1,0:T(8,128)}) custom-call(f32[1]{0:T(128)} %bitcast.2.scale, bf16[816,7000]{1,0:T(8,128)(2,1)} %get-tuple-element.42.d_ref, bf16[816,1024]{1,0:T(8,128)(2,1)} %get-tuple-element.43.a_ref, ...), custom_call_target="tpu_custom_call" | custom-call | flops 34406400000 | bytes 70000000 | tf_op jit(solution)/shard_map/output_layer/pallas_call | solution.py:65
  282.3 66.2 %hidden_backward.1 = (bf16[800,1024]{1,0:T(8,128)(2,1)}, bf16[1936,800]{1,0:T(8,128)(2,1)}, f32[8,128]{1,0:T(8,128)}) custom-call(f32[816,1024]{1,0:T(8,128)} %get-tuple-element.45.g4, f32[800,1024]{1,0:T(8,128)} %get-tuple-element.46.lin4, bf16[800,800]{1,0:T(8,128)(2,1)} %get-tuple-element.47.w2, bf16[800,256]{1,0:T(8,128)(2,1)} %get-tuple-element.48.wh, ...), custom_call_target="tpu_custom_call" | custom-call | tf_op jit(solution)/shard_map/hidden_backward/pallas_call | solution.py:833
  348.5 38.4 %last_layer.1 = (bf16[8928,800]{1,0:T(8,128)(2,1)}, bf16[7000,1024]{1,0:T(8,128)(2,1)}) custom-call(bf16[7000,1024]{1,0:T(8,128)(2,1)} %bitcast.11, bf16[8928,800]{1,0:T(8,128)(2,1)} %get-tuple-element.40.F.w_ref, bf16[800,1024]{1,0:T(8,128)(2,1)} %get-tuple-element.62.d_ref, bf16[7000,1024]{1,0:T(8,128)(2,1)} %get-tuple-element.63.t_ref), custom_call_target="tpu_custom_call" | custom-call | flops 22937600000 | bytes 70000000 | tf_op jit(solution)/shard_map/last_layer/pallas_call | solution.py:122
  386.9 2.0 slice_dynamic-update-slice_fusion.FG
  388.9 148.7 %sum_gradients.1 = (f32[496,800]{1,0:T(8,128)}, f32[64,7000]{1,0:T(8,128)}, f32[32,800]{1,0:T(8,128)}, f32[16,7000]{1,0:T(8,128)}) custom-call(bf16[8928,800]{1,0:T(8,128)(2,1)} %slice_dynamic-update-slice_fusion.FG, bf16[816,7000]{1,0:T(8,128)(2,1)} %get-tuple-element.67.DG), custom_call_target="tpu_custom_call" | custom-call | tf_op jit(solution)/shard_map/sum_gradients/pallas_call | solution.py:1050
  537.6 2.6 reshape.43
  540.2 1.2 slice.44
  541.4 2.7 reshape.45
  544.1 2.0 reshape.44
  547.1 1.6 slice.41
  548.7 1.2 slice.37
  553.3 4.8 fusion.1
  (20 shorter events, 5.9 us)
Async XLA Ops:
  0.6 13.2 %copy-start.1 = (bf16[397952]{0:T(1024)(128)(2,1)S(1)}, bf16[397952]{0:T(1024)(128)(2,1)}, u32[]{:S(2)}) copy-start(bf16[397952]{0:T(1024)(128)(2,1)} %param.7) | copy-start | bytes 2387716
  1.7 12.1 %collective-permute-start.1 = (bf16[112000]{0:T(1024)(128)(2,1)S(1)}, bf16[112000]{0:T(1024)(128)(2,1)S(1)}, u32[]{:S(2)}, u32[]{:S(2)}) collective-permute-start(bf16[112000]{0:T(1024)(128)(2,1)S(1)} %slice.34), channel_id=1, source_target_pairs={{1,0},{2,1},{3,2},{4,3},{5,4},{6,5},{7,6},{8,7},{9,8},{10,9},{11,1... | collective-permute-start | bytes 672008 | tf_op jit(solution)/shard_map/ppermute | solution.py:456
  5.2 8.6 %collective-permute-start = (bf16[36864]{0:T(1024)(128)(2,1)S(1)}, bf16[36864]{0:T(1024)(128)(2,1)S(1)}, u32[]{:S(2)}, u32[]{:S(2)}) collective-permute-start(bf16[36864]{0:T(1024)(128)(2,1)S(1)} %slice.33), channel_id=1, source_target_pairs={{0,1},{1,2},{2,3},{3,4},{4,5},{5,6},{6,7},{7,8},{8,9},{9,10},{10,1... | collective-permute-start | bytes 221192 | tf_op jit(solution)/shard_map/ppermute | solution.py:455
  348.5 38.4 %copy-start = (bf16[1936,800]{1,0:T(8,128)(2,1)S(1)}, bf16[1936,800]{1,0:T(8,128)(2,1)}, u32[]{:S(2)}) copy-start(bf16[1936,800]{1,0:T(8,128)(2,1)} %get-tuple-element.66) | copy-start | bytes 9292804
  541.4 9.8 %copy-start.2 = (f32[8,128]{1,0:T(8,128)S(1)}, f32[8,128]{1,0:T(8,128)}, u32[]{:S(2)}) copy-start(f32[8,128]{1,0:T(8,128)} %get-tuple-element.41.table) | copy-start | bytes 12292

commit v4 on v3

--- a/solution.py
+++ b/solution.py
@@ -845,7 +845,7 @@
 
 ZF, ZD = (0, 1, 2), (2, 3)
 
-def reduce_kernel(FG, DG, fo, do, nf, pd, tF, tD, cF, cD, rF, rD, aF, aD, bF, bD, uF, uD, vF, vD, send, recv, loc, hsend, hrecv):
+def reduce_kernel(FG, DG, fo, do, nf, pd, tF, tD, cF, cD, rF, rD, gF, gD, hF, hD, aF, aD, bF, bD, uF, uD, vF, vD, send, recv, loc, hsend, hrecv):
     z, x, y, c = place()
     XP, YP, CP = (z, 1 - x, y, c), (z, x, 1 - y, c), (z, x, y, 1 - c)
     UP, DN = (z + 1, x, y, c), (z - 1, x, y, c)
@@ -909,11 +909,13 @@
         for cond, cp in make(*a):
             grd(cond, guard, cp.wait_recv)
 
-    def each(rows, off, fn):
+    def each(rows, off, step, fn):
         def body(i, _):
-            fn(pl.ds(pl.multiple_of(off + 16 * i, 16), 16))
+            fn(pl.ds(pl.multiple_of(off + step * i, 16), step))
             return 0
-        lax.fori_loop(0, rows // 16, body, 0)
+        lax.fori_loop(0, rows // step, body, 0)
+        if rows % step:
+            fn(pl.ds(off + rows - rows % step, rows % step))
 
     def total(s, guard, part, zz, dst, terms, out=None):
         for cond, b, off, rows, q in cases(s, part):
@@ -928,10 +930,10 @@
                         dst(b, zc)[0][r, :] = v.astype(jnp.bfloat16)
                     else:
                         out[0 if b == "F" else 1][r, :] = v
-                each(rows, off, step)
+                each(rows, off, 80 if b == "F" else 16, step)
             grd(cond, guard, fn)
 
-    C, R, A, B, U, V = (cF, cD), (rF, rD), (aF, aD), (bF, bD), (uF, uD), (vF, vD)
+    C, R, GU, GD, A, B, U, V = (cF, cD), (rF, rD), (gF, gD), (hF, hD), (aF, aD), (bF, bD), (uF, uD), (vF, vD)
     cols = ((x, y), (1 - x, y), (x, 1 - y), (1 - x, 1 - y))
     tags = [(7, z - 3, z >= 3), (6, z + 3, z <= 0), (5, z - 2, z >= 2), (4, z + 2, z <= 1),
             (3, z - 1, z >= 1), (2, z + 1, z <= 2), (0, z, None)]
@@ -967,23 +969,50 @@
         mine = lambda b, zc: ((tF if b == "F" else tD).at[k % 2], 0)
         total(s, guard, "all", zz, on(C, col), [on(C, col), mine])
 
+    distance = {7: 3, 6: 3, 5: 2, 4: 2, 3: 1, 2: 1, 0: 0}
+    also = lambda guard, cond: cond if guard is None else jnp.logical_and(guard, cond)
+
+    def by_z(s, t, zz):
+        has = lambda planes: lax.bitwise_and(lax.shift_right_arithmetic(planes, jnp.clip(zz, 0, 3)), 1) == 1
+        return [jnp.where(s < NF, has(f).astype(jnp.int32), has(d).astype(jnp.int32)) == 1
+                for f, d in zip(Spread.VIA["F"][t], Spread.VIA["D"][t])]
+
+    def flat(s, t, zz, guard):
+        return [also(guard, jnp.logical_not(v)) for v in by_z(s, t, zz)] if t else [guard, guard]
+
     def first(i):
         tag, zz, guard = tags[i]
+        t, down = distance[tag], tag in (7, 5, 3)
         join(4 * i)
         s = index(zz, *cols[3], c)
-        go(guard, s, zz, "a", ("xa", tag), XP, on(C, 3), on(R, 1))
-        go(guard, s, zz, "b", ("yb", tag), YP, on(C, 3), on(R, 0))
+        sides = [(UP, GU, "hd", z < 3)] if down or t == 0 else []
+        sides += [(DN, GD, "hu", z > 0)] if not down or t == 0 else []
+        for frm, pair, name, more in sides if t < 3 else []:
+            for part, v in zip("ab", by_z(s, t + 1, zz)):
+                g = also(guard, jnp.logical_and(more, v))
+                got(g, s, zz, part, (name, t + 1, part), frm, on(C, 3), on(pair))
+                total(s, g, part, zz, on(C, 3), [on(C, 3), on(pair)])
+        if t:
+            to, pair, name = (DN, GU, "hd") if down else (UP, GD, "hu")
+            for part, v in zip("ab", by_z(s, t, zz)):
+                go(also(guard, v), s, zz, part, (name, t, part), to, on(C, 3), on(pair))
+        near_a, near_b = flat(s, t, zz, guard)
+        go(near_a, s, zz, "a", ("xa", tag), XP, on(C, 3), on(R))
+        go(near_b, s, zz, "b", ("yb", tag), YP, on(C, 3), on(R))
         for k in (1, 2, 3):
             join(4 * i + k)
 
     def second(i):
         tag, zz, guard = tags[i]
+        t = distance[tag]
         sx, sy = index(zz, *cols[1], c), index(zz, *cols[2], c)
-        got(guard, sx, zz, "b", ("yb", tag), YP, on(C, 3), on(R, 0))
-        total(sx, guard, "b", zz, on(C, 1), [on(C, 1), on(R, 0)])
+        near = flat(sx, t, zz, guard)[1]
+        got(near, sx, zz, "b", ("yb", tag), YP, on(C, 3), on(R))
+        total(sx, near, "b", zz, on(C, 1), [on(C, 1), on(R)])
         go(guard, sx, zz, "all", ("X", tag), XP, on(C, 1), on(A))
-        got(guard, sy, zz, "a", ("xa", tag), XP, on(C, 3), on(R, 1))
-        total(sy, guard, "a", zz, on(C, 2), [on(C, 2), on(R, 1)])
+        near = flat(sy, t, zz, guard)[0]
+        got(near, sy, zz, "a", ("xa", tag), XP, on(C, 3), on(R))
+        total(sy, near, "a", zz, on(C, 2), [on(C, 2), on(R)])
         go(guard, sy, zz, "all", ("Y", tag), YP, on(C, 2), on(B))
 
     def third(i):
@@ -991,7 +1020,7 @@
         s = index(zz, *cols[0], c)
         got(guard, s, zz, "all", ("X", tag), XP, on(C, 1), on(A))
         got(guard, s, zz, "all", ("Y", tag), YP, on(C, 2), on(B))
-        t = {7: 3, 6: 3, 5: 2, 4: 2, 3: 1, 2: 1, 0: 0}[tag]
+        t = distance[tag]
         base = [on(C, 0), on(A), on(B)]
         if t == 0:
             for cond, frm, pair, key in ((z < 3, UP, U, ("zd", 1)), (z > 0, DN, V, ("zu", 1))):
@@ -1053,7 +1082,7 @@
                    jax.ShapeDtypeStruct((32, 800), jnp.float32), jax.ShapeDtypeStruct((16, 7000), jnp.float32)),
         in_specs=[pl.BlockSpec(memory_space=pl.ANY)] * 2,
         out_specs=[pl.BlockSpec(memory_space=V)] * 4,
-        scratch_shapes=[V((2, FROWS, 800), B16), V((2, DROWS, 7000), B16), *pair(4), *pair(2), *pair(), *pair(), *pair(), *pair(),
+        scratch_shapes=[V((2, FROWS, 800), B16), V((2, DROWS, 7000), B16), *pair(4), *[b for _ in range(7) for b in pair()],
                         pltpu.SemaphoreType.DMA((192,)), pltpu.SemaphoreType.DMA((192,)), pltpu.SemaphoreType.DMA((2, 2)),
                         pltpu.SemaphoreType.DMA((3,)), pltpu.SemaphoreType.DMA((3,))],
         compiler_params=pltpu.CompilerParams(collective_id=cid, has_side_effects=True, vmem_limit_bytes=60 * 2**20),

time: 570 us -> 562 us (0.986)
  the two profiles are of different devices: /device:TPU:17 before, /device:TPU:31 now
where the time goes in v4:
time: 562 us; the launch traced here: 553 us
  Pallas kernels  506 us (90%)
  local copies, waits for them, and re-layouts  26.2 us (5%)
  other arithmetic  10.2 us (2%)
  between operations  6.58 us (1%)
    pallas_call x1, Pallas kernels, reduce(): pl.pallas_call(reduce_kernel, out_shape=(jax.ShapeDtypeStruct((FROWS, 800...  142 us
    pallas_call x1, Pallas kernels, spread_and_first(): pl.pallas_call(first_kernel, out_shape=(jax.ShapeDtypeStruct((FROWS * NF,...  136 us
    pallas_call x1, Pallas kernels, hidden_backward(): pl.pallas_call(functools.partial(backward_kernel, total), out_shape=(S((H...  66.1 us
    pallas_call x1, Pallas kernels, output_layer(): pl.pallas_call(functools.partial(output_kernel, part, block), grid=(n,),...  65.1 us
    pallas_call x1, Pallas kernels, hidden_layers(): pl.pallas_call(functools.partial(forward_kernel, total), out_shape=(S((H,...  58 us
    pallas_call x1, Pallas kernels, last_layer(): pl.pallas_call(last_kernel, grid=(pl.cdiv(G, block),), out_shape=(jax.Sha...  38.4 us
  transfers between devices with their start and end apart: 2, of which 0 were waited for; matrix products, arithmetic and copies ran while one was open for 1% of the time, Pallas kernels for 0%

profile of v4, /device:TPU:31, one launch (start us, length us, event | category | flops | bytes accessed | tf_op | source)
XLA Modules:
  0.0 552.8 jit_solution(4873686074494382519)
XLA Ops:
  0.6 1.0 slice.34
  1.7 2.6 collective-permute-start.1
  5.2 1.3 collective-permute-start
  6.5 1.3 fusion.4.hot.h_ref
  7.8 1.5 convert_element_type.13.p_ref
  9.3 1.7 pad.4.eps
  11.0 1.1 convert_reduce_fusion
  12.7 2.3 reshape.41.ds
  15.5 2.2 reshape.40.fs
  17.8 136.1 %spread_and_first.1 = (bf16[8928,800]{1,0:T(8,128)(2,1)}, bf16[816,7000]{1,0:T(8,128)(2,1)}, f32[800,1024]{1,0:T(8,128)}) custom-call(bf16[496,800]{1,0:T(8,128)(2,1)} %reshape.40.fs, bf16[7000,1024]{1,0:T(8,128)(2,1)} %bitcast.9, bf16[64,7000]{1,0:T(8,128)(2,1)} %reshape.41.ds), custom_call_target="tpu_custom_call" | custom-call | tf_op jit(solution)/shard_map/spread_and_first/pallas_call | solution.py:438
  153.9 58.0 %hidden_layers.1 = (bf16[800,800]{1,0:T(8,128)(2,1)}, bf16[800,256]{1,0:T(8,128)(2,1)}, bf16[128,800]{1,0:T(8,128)(2,1)}, bf16[800,800]{1,0:T(8,128)(2,1)}, f32[...) custom-call(f32[800,1024]{1,0:T(8,128)} %get-tuple-element.39.lin1.l, ...), custom_call_target="tpu_custom_call" | custom-call | tf_op jit(solution)/shard_map/hidden_layers/pallas_call | solution.py:682
  212.7 1.2 slice.38
  215.9 65.1 %output_layer.1 = (bf16[7000,1024]{1,0:T(8,128)(2,1)}, bf16[7000,1024]{1,0:T(8,128)(2,1)}, bf16[816,7000]{1,0:T(8,128)(2,1)}, f32[816,1024]{1,0:T(8,128)}, f32[8,1024]{1,0:T(8,128)}) custom-call(f32[1]{0:T(128)} %bitcast.2.scale, bf16[816,7000]{1,0:T(8,128)(2,1)} %get-tuple-element.42.d_ref, bf16[816,1024]{1,0:T(8,128)(2,1)} %get-tuple-element.43.a_ref, ...), custom_call_target="tpu_custom_call" | custom-call | flops 34406400000 | bytes 70000000 | tf_op jit(solution)/shard_map/output_layer/pallas_call | solution.py:65
  281.0 66.1 %hidden_backward.1 = (bf16[800,1024]{1,0:T(8,128)(2,1)}, bf16[1936,800]{1,0:T(8,128)(2,1)}, f32[8,128]{1,0:T(8,128)}) custom-call(f32[816,1024]{1,0:T(8,128)} %get-tuple-element.45.g4, f32[800,1024]{1,0:T(8,128)} %get-tuple-element.46.lin4, bf16[800,800]{1,0:T(8,128)(2,1)} %get-tuple-element.47.w2, bf16[800,256]{1,0:T(8,128)(2,1)} %get-tuple-element.48.wh, ...), custom_call_target="tpu_custom_call" | custom-call | tf_op jit(solution)/shard_map/hidden_backward/pallas_call | solution.py:833
  347.2 38.4 %last_layer.1 = (bf16[8928,800]{1,0:T(8,128)(2,1)}, bf16[7000,1024]{1,0:T(8,128)(2,1)}) custom-call(bf16[7000,1024]{1,0:T(8,128)(2,1)} %bitcast.11, bf16[8928,800]{1,0:T(8,128)(2,1)} %get-tuple-element.40.F.w_ref, bf16[800,1024]{1,0:T(8,128)(2,1)} %get-tuple-element.62.d_ref, bf16[7000,1024]{1,0:T(8,128)(2,1)} %get-tuple-element.63.t_ref), custom_call_target="tpu_custom_call" | custom-call | flops 22937600000 | bytes 70000000 | tf_op jit(solution)/shard_map/last_layer/pallas_call | solution.py:122
  385.5 2.0 slice_dynamic-update-slice_fusion.FG
  387.6 142.3 %sum_gradients.1 = (f32[496,800]{1,0:T(8,128)}, f32[64,7000]{1,0:T(8,128)}, f32[32,800]{1,0:T(8,128)}, f32[16,7000]{1,0:T(8,128)}) custom-call(bf16[8928,800]{1,0:T(8,128)(2,1)} %slice_dynamic-update-slice_fusion.FG, bf16[816,7000]{1,0:T(8,128)(2,1)} %get-tuple-element.67.DG), custom_call_target="tpu_custom_call" | custom-call | tf_op jit(solution)/shard_map/sum_gradients/pallas_call | solution.py:1079
  529.8 2.6 reshape.43
  532.5 1.2 slice.44
  533.7 2.7 reshape.45
  536.4 2.0 reshape.44
  539.4 1.6 slice.41
  541.0 1.2 slice.37
  545.6 4.8 fusion.1
  (20 shorter events, 5.9 us)
Async XLA Ops:
  0.6 11.5 %copy-start.1 = (bf16[397952]{0:T(1024)(128)(2,1)S(1)}, bf16[397952]{0:T(1024)(128)(2,1)}, u32[]{:S(2)}) copy-start(bf16[397952]{0:T(1024)(128)(2,1)} %param.7) | copy-start | bytes 2387716
  1.7 10.4 %collective-permute-start.1 = (bf16[112000]{0:T(1024)(128)(2,1)S(1)}, bf16[112000]{0:T(1024)(128)(2,1)S(1)}, u32[]{:S(2)}, u32[]{:S(2)}) collective-permute-start(bf16[112000]{0:T(1024)(128)(2,1)S(1)} %slice.34), channel_id=1, source_target_pairs={{1,0},{2,1},{3,2},{4,3},{5,4},{6,5},{7,6},{8,7},{9,8},{10,9},{11,1... | collective-permute-start | bytes 672008 | tf_op jit(solution)/shard_map/ppermute | solution.py:456
  5.2 6.9 %collective-permute-start = (bf16[36864]{0:T(1024)(128)(2,1)S(1)}, bf16[36864]{0:T(1024)(128)(2,1)S(1)}, u32[]{:S(2)}, u32[]{:S(2)}) collective-permute-start(bf16[36864]{0:T(1024)(128)(2,1)S(1)} %slice.33), channel_id=1, source_target_pairs={{0,1},{1,2},{2,3},{3,4},{4,5},{5,6},{6,7},{7,8},{8,9},{9,10},{10,1... | collective-permute-start | bytes 221192 | tf_op jit(solution)/shard_map/ppermute | solution.py:455
  347.2 38.4 %copy-start = (bf16[1936,800]{1,0:T(8,128)(2,1)S(1)}, bf16[1936,800]{1,0:T(8,128)(2,1)}, u32[]{:S(2)}) copy-start(bf16[1936,800]{1,0:T(8,128)(2,1)} %get-tuple-element.66) | copy-start | bytes 9292804
  533.7 9.8 %copy-start.2 = (f32[8,128]{1,0:T(8,128)S(1)}, f32[8,128]{1,0:T(8,128)}, u32[]{:S(2)}) copy-start(f32[8,128]{1,0:T(8,128)} %get-tuple-element.41.table) | copy-start | bytes 12292
